TPU v7x, 256 devices: a whole 4x4x8 slice. The times are simulated.
256 devices in a mesh: dp: 32 (over z, x), tensor: 8 (over y, core).
Axes of the slice: x: 4, y: 4, z: 8, core: 2. Of those that a mesh axis runs over, the one named last changes fastest.
Arguments:
- queries: bfloat16 [16384, 8192], P('dp', 'tensor'), may hold values from -16 to 16
- key_rows: bfloat16 [16384, 1024], P('dp', 'tensor'), may hold values from -16 to 16
- value_matrix: bfloat16 [16384, 1024], P('dp', 'tensor'), may hold values from -6 to 6
- out_grad: bfloat16 [16384, 8192], P('dp', 'tensor'), may hold values from -6 to 6
- inputs: bfloat16 [16384, 8192], P('dp', 'tensor'), may hold values from -0.08984375 to 0.08984375
- doc_ids: int32 [16384], replicated, may hold values from 0 to 127, never falling along the last dimension, each value on 1 to 256 neighbouring positions
Outputs:
- attention_out: bfloat16 [16384, 8192], P('dp', 'tensor')
- query_grad: bfloat16 [16384, 8192], P('dp', 'tensor')
- key_gradient: bfloat16 [16384, 1024], P('dp', 'tensor')
- value_gradient: bfloat16 [16384, 1024], P('dp', 'tensor')
- softmax_logsum: float32 [64, 16384], P('tensor', 'dp')
- projection_weight_gradient: float32 [8192, 2048], P(('tensor', 'dp'))
Inputs may be any that keep to these rules, and one draw needn't show every extreme that they name: `doc_ids`: document numbers never fall along the rows; each document is 1 to 256 consecutive rows, and some document has exactly 256.
All inputs are finite; a program needn't handle non-finite values.
Results may differ from a plain program's by a relative error of at most 0.02.
Values may be sent and summed in bfloat16 or wider, within the bound.
No kernel may reach another device: no remote copies, remote signals or barrier semaphores. Data moves between devices by JAX's collectives and lax.ppermute only.
A program may use at most 64 MiB of HBM per device.

v0:
```python
import jax
import jax.numpy as jnp
from jax import lax
from jax.sharding import PartitionSpec as P

HEAD_SIZE = 128


def passed_along(value, axis, steps):
    count = lax.axis_size(axis)
    leading, last = (max(0, -steps), min(count, count - steps))
    return lax.ppermute(value, axis, [(source, source + steps) for source in range(leading, last)])


def attend_head(query_rows, key_block, val_block, grad_rows, allowed):
    score_scale = query_rows.shape[-1] ** (-0.5)
    scores = (
        jnp.einsum("rd,cd->rc", query_rows, key_block, preferred_element_type=jnp.float32)
        * score_scale
    )
    masked = jnp.where(allowed, scores, -jnp.inf)
    row_max = jnp.max(masked, axis=-1)
    expd = jnp.where(allowed, jnp.exp(masked - row_max[:, None]), 0.0)
    totals = jnp.sum(expd, axis=-1)
    probs = expd / totals[:, None]
    logsum = row_max + jnp.log(totals)
    probs_low = probs.astype(jnp.bfloat16)
    out_rows = jnp.einsum(
        "rc,cd->rd", probs_low, val_block, preferred_element_type=jnp.float32
    ).astype(jnp.bfloat16)
    out_rows = lax.optimization_barrier(out_rows)
    delta = jnp.sum(grad_rows.astype(jnp.float32) * out_rows.astype(jnp.float32), axis=-1)
    dprobs = jnp.einsum("rd,cd->rc", grad_rows, val_block, preferred_element_type=jnp.float32)
    dscores = (score_scale * probs * (dprobs - delta[:, None])).astype(jnp.bfloat16)
    query_grad = jnp.einsum(
        "rc,cd->rd", dscores, key_block, preferred_element_type=jnp.float32
    ).astype(jnp.bfloat16)
    key_part = jnp.einsum("rc,rd->cd", dscores, query_rows, preferred_element_type=jnp.float32)
    value_part = jnp.einsum("rc,rd->cd", probs_low, grad_rows, preferred_element_type=jnp.float32)
    return (out_rows, query_grad, key_part, value_part, logsum)


def kv_head(query_heads, grad_heads, key_block, val_block, allowed):

    def step(totals, pieces):
        out_one, dq_one, key_part, value_part, lse_one = attend_head(
            pieces[0], key_block, val_block, pieces[1], allowed
        )
        return ((totals[0] + key_part, totals[1] + value_part), (out_one, dq_one, lse_one))

    empty = jnp.zeros(key_block.shape, jnp.float32)
    sums, stacked = lax.scan(step, (empty, empty), (query_heads, grad_heads))
    return (stacked[0], stacked[1], sums[0], sums[1], stacked[2])


def body(queries, key_rows, value_matrix, out_grad, inputs, doc_ids):
    my_shard = lax.axis_index("dp")
    tok_rows = queries.shape[0]
    kv_local = key_rows.shape[1] // HEAD_SIZE
    group_width = queries.shape[1] // key_rows.shape[1]
    first = my_shard * tok_rows
    row_ids = jnp.arange(tok_rows, dtype=jnp.int32)
    own_seg = lax.dynamic_slice_in_dim(doc_ids, first, tok_rows)
    own_pos = first + row_ids
    span_ids = jnp.arange(tok_rows, dtype=jnp.int32)
    prior_pos = first - tok_rows + span_ids
    prior_seg = jnp.where(
        my_shard > 0,
        lax.dynamic_slice_in_dim(doc_ids, jnp.maximum(first - tok_rows, 0), tok_rows),
        -1,
    )
    prior_keys, prior_vals = passed_along((key_rows, value_matrix), "dp", 1)
    query_heads = queries.reshape(tok_rows, kv_local, group_width, HEAD_SIZE).transpose(1, 2, 0, 3)
    grad_heads = out_grad.reshape(tok_rows, kv_local, group_width, HEAD_SIZE).transpose(1, 2, 0, 3)
    all_heads = jax.vmap(kv_head, in_axes=(0, 0, 1, 1, None))
    key_block = jnp.concatenate([prior_keys, key_rows], axis=0)
    key_count = key_block.shape[0]
    allowed = (own_seg[:, None] == jnp.concatenate([prior_seg, own_seg])[None, :]) & (
        jnp.concatenate([prior_pos, own_pos])[None, :] <= own_pos[:, None]
    )
    out_rows, q_grad, k_sum, v_sum, logsum = all_heads(
        query_heads,
        grad_heads,
        key_block.reshape(key_count, kv_local, HEAD_SIZE),
        jnp.concatenate([prior_vals, value_matrix], axis=0).reshape(key_count, kv_local, HEAD_SIZE),
        allowed,
    )
    out_flat = out_rows.transpose(2, 0, 1, 3).reshape(tok_rows, -1)
    dq_flat = q_grad.transpose(2, 0, 1, 3).reshape(tok_rows, -1)
    k_flat = k_sum.transpose(1, 0, 2).reshape(key_count, -1)
    v_flat = v_sum.transpose(1, 0, 2).reshape(key_count, -1)
    out_flat, dq_flat, k_flat, v_flat, logsum = (
        out_flat,
        dq_flat,
        k_flat,
        v_flat,
        logsum.reshape(kv_local * group_width, tok_rows),
    )
    results = (
        out_flat,
        dq_flat,
        k_flat[:tok_rows],
        k_flat[tok_rows:],
        v_flat[:tok_rows],
        v_flat[tok_rows:],
        logsum,
    )
    attention_out, query_grad, key_prior, key_own, value_prior, value_own, softmax_logsum = results
    key_back, value_back = (
        passed_along(key_prior.astype(jnp.bfloat16), "dp", -1).astype(key_prior.dtype),
        passed_along(value_prior.astype(jnp.bfloat16), "dp", -1).astype(value_prior.dtype),
    )
    tail = tok_rows - tok_rows
    key_gradient = jnp.concatenate([key_own[:tail], key_own + key_back], axis=0).astype(
        jnp.bfloat16
    )
    value_gradient = jnp.concatenate([value_own[:tail], value_own + value_back], axis=0).astype(
        jnp.bfloat16
    )
    key_value_joined = jnp.stack(
        [
            key_gradient.reshape(tok_rows, kv_local, HEAD_SIZE),
            value_gradient.reshape(tok_rows, kv_local, HEAD_SIZE),
        ],
        axis=2,
    ).reshape(tok_rows, -1)
    kv_all = lax.all_gather(key_value_joined, "tensor", axis=1, tiled=True)
    projection_weight_gradient = lax.psum_scatter(
        lax.dot_general(
            inputs, kv_all, (((0,), (0,)), ((), ())), preferred_element_type=jnp.float32
        ).astype(jnp.bfloat16),
        "dp",
        scatter_dimension=0,
        tiled=True,
    ).astype(jnp.float32)
    return (
        attention_out,
        query_grad,
        key_gradient,
        value_gradient,
        softmax_logsum,
        projection_weight_gradient,
    )


def solution(mesh):
    in_specs = (
        P("dp", "tensor"),
        P("dp", "tensor"),
        P("dp", "tensor"),
        P("dp", "tensor"),
        P("dp", "tensor"),
        P(),
    )
    out_specs = (
        P("dp", "tensor"),
        P("dp", "tensor"),
        P("dp", "tensor"),
        P("dp", "tensor"),
        P("tensor", "dp"),
        P(("tensor", "dp"), None),
    )
    return jax.shard_map(body, mesh=mesh, in_specs=in_specs, out_specs=out_specs, check_vma=False)
```

profile of v0, /device:TPU:2, one launch (start us, length us, event | category | flops | bytes accessed | tf_op | source)
XLA Modules:
  0.0 409.6 jit_solution(18162725016781144873)
XLA Ops:
  7.2 3.5 collective-permute-start
  10.8 3.1 collective-permute-start.1
  14.8 1.5 copy.28
  16.4 2.3 copy.29
  18.8 102.8 %while.19 = (s32[]{:T(128)}, f32[1,1024,128]{2,1,0:T(8,128)}, f32[1,1024,128]{2,1,0:T(8,128)}, bf16[8,1,512,128]{3,2,1,0:T(8,128)(2,1)}, bf16[8,1,512,128]{3,2,1...) while((s32[]{:T(128)}, f32[1,1024,128]{2,1,0:T(8,128)}, ...), condition=%wide.region_4.5_spmd.clone, body=%wide.region_0.4_spmd.clone.sunk | while | flops 820902912 | bytes 42267064 | solution.py:52
  18.8 1.1 constant_dynamic-slice_fusion.2
  23.9 1.3 dynamic_update_slice.21
  28.2 1.6 fusion.69
  29.9 1.1 fusion.71
  31.6 1.1 constant_dynamic-slice_fusion.2
  36.7 1.3 dynamic_update_slice.21
  41.1 1.6 fusion.69
  42.7 1.1 fusion.71
  44.5 1.1 constant_dynamic-slice_fusion.2
  49.5 1.3 dynamic_update_slice.21
  53.9 1.6 fusion.69
  55.6 1.1 fusion.71
  62.4 1.3 dynamic_update_slice.21
  66.7 1.6 fusion.69
  68.4 1.1 fusion.71
  70.2 1.1 constant_dynamic-slice_fusion.2
  75.2 1.3 dynamic_update_slice.21
  79.6 1.6 fusion.69
  81.2 1.1 fusion.71
  83.0 1.1 constant_dynamic-slice_fusion.2
  88.1 1.3 dynamic_update_slice.21
  92.5 1.6 fusion.69
  94.1 1.1 fusion.71
  95.9 1.1 constant_dynamic-slice_fusion.2
  100.9 1.3 dynamic_update_slice.21
  105.3 1.6 fusion.69
  106.9 1.1 fusion.71
  113.8 1.3 dynamic_update_slice.21
  118.1 1.6 fusion.69
  119.8 1.1 fusion.71
  121.6 1.2 copy.34
  122.8 2.7 collective-permute-start.2
  125.6 1.2 copy.36
  126.9 1.9 collective-permute-start.3
  129.7 4.0 collective-permute-done.3
  134.6 32.8 %all-gather.2.cloned.1.call-done = bf16[512,2048]{0,1:T(8,128)(2,1)} async-done(((bf16[512,256]{0,1:T(8,128)(2,1)}), bf16[512,2048]{0,1:T(8,128)(2,1)}) %all-gather.2.cloned.1.call-update) | async-done | bytes 2097168 | tf_op jit(solution)/shard_map/all_gather | solution.py:127
  167.4 5.9 %convert_bitcast_fusion = bf16[1024,2048]{0,1:T(8,128)(2,1)} fusion(bf16[512,2048]{0,1:T(8,128)(2,1)} %all-gather.2.cloned.1.call-done, bf16[512,1024]{1,0:T(8,128)(2,1)S(1)} %copy-done), kind=kOutput, calls=%fused_computation.37 | convolution fusion | flops 2149580800 | bytes 7340032 | tf_op jit(solution)/shard_map/dot_general | solution.py:129
  173.3 6.6 %copy.41 = bf16[1024,2048]{1,0:T(8,128)(2,1)} copy(bf16[1024,2048]{0,1:T(8,128)(2,1)} %convert_bitcast_fusion) | data formatting | bytes 8388608
  179.9 1.2 copy-done.11
  181.8 1.2 copy.53
  183.7 1.2 copy.52
  186.5 214.2 %reduce-scatter.4.cloned.1.call-done = bf16[32,2048]{1,0:T(8,128)(2,1)} async-done(((bf16[1024,2048]{1,0:T(8,128)(2,1)}), bf16[32,2048]{1,0:T(8,128)(2,1)}) %reduce-scatter.4.cloned.1.call-update) | async-done | bytes 131088
  400.7 1.2 copy.42
  (263 shorter events, 69.8 us)
Async XLA Ops:
  7.2 160.2 %copy-start = (bf16[512,1024]{1,0:T(8,128)(2,1)S(1)}, bf16[512,1024]{1,0:T(8,128)(2,1)}, u32[]{:S(2)}) copy-start(bf16[512,1024]{1,0:T(8,128)(2,1)} %param.12) | copy-start | bytes 3145732
  7.2 160.2 %all-gather.2.cloned.1.call-start = ((), (), s32[]{:S(2)}) async-start(), calls=%async_computation.1 | async-start | bytes 2359296 | tf_op jit(solution)/shard_map/all_gather | solution.py:127
  7.2 11.5 %collective-permute-start = (bf16[512,128]{1,0:T(8,128)(2,1)}, bf16[512,128]{1,0:T(8,128)(2,1)S(1)}, u32[]{:S(2)}, u32[]{:S(2)}) collective-permute-start(bf16[512,128]{1,0:T(8,128)(2,1)} %param.9), channel_id=1, source_target_pairs={{0,8},{8,16},{16,24},{24,32},{32,40},{40,48},{48,56},{56,64},{64,7... | collective-permute-start | bytes 393224 | tf_op jit(solution)/shard_map/ppermute | solution.py:12
  10.8 7.9 %collective-permute-start.1 = (bf16[512,128]{1,0:T(8,128)(2,1)}, bf16[512,128]{1,0:T(8,128)(2,1)S(1)}, u32[]{:S(2)}, u32[]{:S(2)}) collective-permute-start(bf16[512,128]{1,0:T(8,128)(2,1)} %param.10), channel_id=1, source_target_pairs={{0,8},{8,16},{16,24},{24,32},{32,40},{40,48},{48,56},{56,64},{64,7... | collective-permute-start | bytes 393224 | tf_op jit(solution)/shard_map/ppermute | solution.py:12
  14.8 3.9 copy-start.12
  14.8 3.9 copy-start.13
  18.8 2.7 copy-start.6
  18.8 2.6 copy-start.8
  27.0 2.9 copy-start.2
  28.2 3.4 copy-start.9
  31.6 2.6 copy-start.6
  31.6 2.6 copy-start.8
  39.8 2.9 copy-start.2
  41.1 3.4 copy-start.9
  42.7 1.8 copy-start.4
  44.5 2.6 copy-start.6
  44.5 2.6 copy-start.8
  52.7 2.9 copy-start.2
  53.9 3.4 copy-start.9
  55.5 1.8 copy-start.4
  57.3 2.6 copy-start.6
  57.3 2.6 copy-start.8
  65.5 2.9 copy-start.2
  66.7 3.4 copy-start.9
  70.2 2.6 copy-start.6
  70.2 2.6 copy-start.8
  78.3 2.9 copy-start.2
  79.6 3.4 copy-start.9
  81.2 1.8 copy-start.4
  83.0 2.6 copy-start.6
  83.0 2.6 copy-start.8
  91.2 2.9 copy-start.2
  92.4 3.4 copy-start.9
  94.1 1.8 copy-start.4
  95.9 2.6 copy-start.6
  95.9 2.6 copy-start.8
  104.1 2.9 copy-start.2
  105.3 3.4 copy-start.9
  106.9 1.8 copy-start.4
  108.7 2.6 copy-start.6
  108.7 2.6 copy-start.8
  116.9 2.9 copy-start.2
  118.1 3.4 copy-start.9
  119.8 1.8 copy-start.4
  122.8 6.9 %collective-permute-start.2 = (bf16[512,128]{0,1:T(8,128)(2,1)S(1)}, bf16[512,128]{0,1:T(8,128)(2,1)S(1)}, u32[]{:S(2)}, u32[]{:S(2)}) collective-permute-start(bf16[512,128]{0,1:T(8,128)(2,1)S(1)} %fusion.30), channel_id=1, source_target_pairs={{8,0},{16,8},{24,16},{32,24},{40,32},{48,40},{56,48},{64,56},{72,6... | collective-permute-start | bytes 393224 | tf_op jit(solution)/shard_map/ppermute | solution.py:12
  126.9 6.9 %collective-permute-start.3 = (bf16[512,128]{0,1:T(8,128)(2,1)S(1)}, bf16[512,128]{0,1:T(8,128)(2,1)S(1)}, u32[]{:S(2)}, u32[]{:S(2)}) collective-permute-start(bf16[512,128]{0,1:T(8,128)(2,1)S(1)} %fusion.31), channel_id=1, source_target_pairs={{8,0},{16,8},{24,16},{32,24},{40,32},{48,40},{56,48},{64,56},{72,6... | collective-permute-start | bytes 393224 | tf_op jit(solution)/shard_map/ppermute | solution.py:12
  134.5 266.1 %reduce-scatter.4.cloned.1.call-start = ((), (), s32[]{:S(2)}) async-start(), calls=%async_computation.2 | async-start | bytes 4325376
  181.1 1.9 copy-start.10
  (35 other events, 43.8 us)
Sparse Core Ops, SparseCore 0:
  134.6 32.7 all-gather.1
  180.0 220.5 reduce-scatter.3
where the time goes:
time: 412 us; the launch traced here: 410 us
  waiting for transfers between devices  252 us (61%)
  local copies, waits for them, and re-layouts  62.2 us (15%)
  matrix products  46.6 us (11%)
  other arithmetic  22.3 us (5%)
  between operations  14.3 us (3%)
  starting transfers between devices  11.4 us (3%)
    unnamed x3, waiting for transfers between devices  214 us
    all_gather x1, waiting for transfers between devices, body(): kv_all = lax.all_gather(key_value_joined, 'tensor', axis=1, tiled=True)  32.8 us
    unnamed x19, local copies, waits for them, and re-layouts  17.7 us
    dynamic_update_slice x16, local copies, waits for them, and re-layouts, kv_head(): sums, stacked = lax.scan(step, (empty, empty), (query_heads, grad_heads))  16 us
    dynamic_slice x16, local copies, waits for them, and re-layouts, kv_head(): sums, stacked = lax.scan(step, (empty, empty), (query_heads, grad_heads))  14.6 us
    dot_general x8, matrix products, attend_head(): jnp.einsum('rc,rd->cd', dscores, query_rows, preferred_element_type=jnp.f...  12.9 us
    ppermute x4, starting transfers between devices, passed_along(): lax.ppermute(value, axis, [(source, source + steps) for source in range(l...  11.3 us
    while x144, local copies, waits for them, and re-layouts  10.1 us
  transfers between devices with their start and end apart: 6, of which 4 were waited for; matrix products, arithmetic and copies ran while one was open for 3% of the time, Pallas kernels for 0%

commit v1 on v0

v1 whole, which is shorter than its diff:
```python
import jax
import jax.numpy as jnp
from jax import lax
from jax.experimental import pallas as pl
from jax.experimental.pallas import tpu as pltpu
from jax.sharding import PartitionSpec as P

HEAD = 128
REACH = 256
BLOCK = 128
WINDOW = REACH + BLOCK
NX, NY, NZ = 4, 4, 8
F32 = jnp.float32
BF16 = jnp.bfloat16
NT = (((1,), (1,)), ((), ()))
TN = (((0,), (0,)), ((), ()))


def dot(a, b, dims=(((1,), (0,)), ((), ()))):
    return lax.dot_general(a, b, dims, preferred_element_type=F32)


def attend_rows(q_ref, g_ref, k_lo, k_hi, v_lo, v_hi, sq_ref, sk_ref, o_ref, dq_ref, lse_ref, dk_ref, dv_ref, p_s, ds_s):
    heads = q_ref.shape[1] // HEAD
    scale = HEAD ** (-0.5)
    keys = jnp.concatenate([k_lo[...], k_hi[...]], axis=0)
    vals = jnp.concatenate([v_lo[...], v_hi[...]], axis=0)
    keys_t = keys.T
    vals_t = vals.T
    dk_ref[...] = jnp.zeros_like(dk_ref)
    dv_ref[...] = jnp.zeros_like(dv_ref)
    for j in range(REACH // BLOCK):
        lo = j * BLOCK
        rows = slice(lo, lo + BLOCK)
        win = slice(lo, lo + WINDOW)
        k_w, v_w = keys[win], vals[win]
        kt_w, vt_w = keys_t[:, win], vals_t[:, win]
        key_at = lax.broadcasted_iota(jnp.int32, (WINDOW, BLOCK), 0)
        query_at = lax.broadcasted_iota(jnp.int32, (WINDOW, BLOCK), 1) + REACH
        allowed = (sk_ref[win, :] == sq_ref[:, rows]) & (key_at <= query_at)
        bias = jnp.where(allowed, 0.0, -1e30).astype(F32)
        bias = jnp.concatenate([bias, bias], axis=1)
        q_parts, g_parts = [], []
        for h in range(0, heads, 2):
            c0 = slice(h * HEAD, (h + 1) * HEAD)
            c1 = slice((h + 1) * HEAD, (h + 2) * HEAD)
            qp = jnp.concatenate([q_ref[rows, c0], q_ref[rows, c1]], axis=0)
            gp = jnp.concatenate([g_ref[rows, c0], g_ref[rows, c1]], axis=0)
            q_parts.append(qp)
            g_parts.append(gp)
            s = dot(k_w, qp, NT) * scale + bias
            top = jnp.max(s, axis=0, keepdims=True)
            e = jnp.exp(s - top)
            total = jnp.sum(e, axis=0, keepdims=True)
            lse = top + jnp.log(total)
            lse_ref[h : h + 1, rows] = lse[:, :BLOCK]
            lse_ref[h + 1 : h + 2, rows] = lse[:, BLOCK:]
            p = e * (1.0 / total)
            dp = dot(v_w, gp, NT)
            delta = jnp.sum(p * dp, axis=0, keepdims=True)
            ds = (p * (dp - delta)).astype(BF16)
            p_low = p.astype(BF16)
            cols = slice(h * BLOCK, (h + 2) * BLOCK)
            p_s[:, cols] = p_low
            ds_s[:, cols] = ds
            o = dot(vt_w, p_low).T
            o_ref[rows, c0] = o[:BLOCK].astype(BF16)
            o_ref[rows, c1] = o[BLOCK:].astype(BF16)
            dq = (dot(kt_w, ds) * scale).T
            dq_ref[rows, c0] = dq[:BLOCK].astype(BF16)
            dq_ref[rows, c1] = dq[BLOCK:].astype(BF16)
        dv_ref[win, :] += dot(p_s[...], jnp.concatenate(g_parts, axis=0))
        dk_ref[win, :] += dot(ds_s[...], jnp.concatenate(q_parts, axis=0)) * scale


def late_kernel(q, g, k_lo, k_hi, v_lo, v_hi, sq, sk, o, dq, lse, dk_out, dv_out, p_s, ds_s):
    attend_rows(q, g, k_lo, k_hi, v_lo, v_hi, sq, sk, o, dq, lse, dk_out, dv_out, p_s, ds_s)


def early_kernel(q, g, k_lo, k_hi, v_lo, v_hi, sq, sk, dk_late, dv_late, o_in, dq_in, lse_in, o, dq, lse, joined, back, p_s, ds_s, dk, dv):
    attend_rows(q, g, k_lo, k_hi, v_lo, v_hi, sq, sk, o, dq, lse, dk, dv, p_s, ds_s)
    back[:, :HEAD] = dk[:REACH].astype(BF16)
    back[:, HEAD:] = dv[:REACH].astype(BF16)
    joined[:, :HEAD] = (dk[REACH:] + dk_late[...]).astype(BF16)
    joined[:, HEAD:] = (dv[REACH:] + dv_late[...]).astype(BF16)


def spec(shape, at):
    return pl.BlockSpec(shape, lambda i: at)


def attention(queries, out_grad, key_rows, value_matrix, prior, seg_own, seg_prior):
    tok, width = queries.shape
    heads = width // HEAD
    half = tok // 2
    seg_row = seg_own.reshape(1, tok)
    seg_col = seg_own.reshape(tok, 1)
    cost = pl.CostEstimate(flops=6 * 2 * half * WINDOW * width, bytes_accessed=4 << 20, transcendentals=half * WINDOW * heads)
    params = pltpu.CompilerParams(vmem_limit_bytes=48 << 20)
    wide = lambda i: spec((half, width), (i, 0))
    kv = lambda i: spec((half, HEAD), (i, 0))
    scratch = [pltpu.VMEM((WINDOW, heads * BLOCK), BF16)] * 2
    rows_out = jax.ShapeDtypeStruct((tok, width), BF16)
    lse_out = jax.ShapeDtypeStruct((heads, tok), F32)
    grad = jax.ShapeDtypeStruct((tok, HEAD), F32)
    o, dq, lse, dk_late, dv_late = pl.pallas_call(
        late_kernel,
        grid=(1,),
        in_specs=[wide(1), wide(1), kv(0), kv(1), kv(0), kv(1), spec((1, half), (0, 1)), spec((tok, 1), (0, 0))],
        out_specs=[wide(1), wide(1), spec((heads, half), (0, 1)), spec((tok, HEAD), (0, 0)), spec((tok, HEAD), (0, 0))],
        out_shape=[rows_out, rows_out, lse_out, grad, grad],
        scratch_shapes=scratch,
        cost_estimate=cost,
        compiler_params=params,
        name="attend_late",
    )(queries, out_grad, key_rows, key_rows, value_matrix, value_matrix, seg_row, seg_col)
    seg_col_early = jnp.concatenate([seg_prior.reshape(half, 1), seg_col[:half]], axis=0)
    hbm = pl.BlockSpec(memory_space=pl.ANY)
    pair = jax.ShapeDtypeStruct((half, 2 * HEAD), BF16)
    o, dq, lse, joined_low, back = pl.pallas_call(
        early_kernel,
        grid=(1,),
        in_specs=[wide(0), wide(0), kv(0), kv(0), spec((half, HEAD), (0, 1)), kv(0), spec((1, half), (0, 0)), spec((tok, 1), (0, 0)),
                  kv(0), kv(0), hbm, hbm, hbm],
        out_specs=[wide(0), wide(0), spec((heads, half), (0, 0)), spec((half, 2 * HEAD), (0, 0)), spec((half, 2 * HEAD), (0, 0))],
        out_shape=[rows_out, rows_out, lse_out, pair, pair],
        scratch_shapes=scratch + [pltpu.VMEM((tok, HEAD), F32)] * 2,
        input_output_aliases={10: 0, 11: 1, 12: 2},
        cost_estimate=cost,
        compiler_params=params,
        name="attend_early",
    )(queries, out_grad, prior, key_rows, prior, value_matrix, seg_row, seg_col_early, dk_late, dv_late, o, dq, lse)
    return o, dq, lse, joined_low, back, dk_late, dv_late


def weight_kernel(core, a0, a1, a3, a2l, a2h, b0, b1, b3, b2, c0, c1, c3, c2, out):
    mine = pl.ds(pl.multiple_of(core[0] * 2 * HEAD, 2 * HEAD), 2 * HEAD)
    other = pl.ds(pl.multiple_of((1 - core[0]) * 2 * HEAD, 2 * HEAD), 2 * HEAD)
    half = a2l.shape[0]
    for cols, (r0, r1, r3, r2) in ((mine, (b0, b1, b3, b2)), (other, (c0, c1, c3, c2))):
        total = dot(a0[...], r0[...], TN) + dot(a1[...], r1[...], TN) + dot(a3[...], r3[...], TN)
        total += dot(a2l[...], r2[:half], TN) + dot(a2h[...], r2[half:], TN)
        out[:, cols] = total.astype(BF16)


def weight_partial(core, a, b, c):
    tok, width = a[0].shape
    tile = 256
    col = lambda rows: pl.BlockSpec((rows, tile), lambda i, core: (0, i))
    whole = pl.BlockSpec((tok, 2 * HEAD), lambda i, core: (0, 0))
    return pl.pallas_call(
        weight_kernel,
        grid_spec=pltpu.PrefetchScalarGridSpec(
            num_scalar_prefetch=1,
            grid=(width // tile,),
            in_specs=[col(tok)] * 3 + [col(tok // 2)] * 2 + [whole] * 8,
            out_specs=pl.BlockSpec((tile, 4 * HEAD), lambda i, core: (i, 0)),
        ),
        out_shape=jax.ShapeDtypeStruct((width, 4 * HEAD), BF16),
        cost_estimate=pl.CostEstimate(flops=2 * width * 4 * HEAD * 4 * tok, bytes_accessed=8 << 20, transcendentals=0),
        compiler_params=pltpu.CompilerParams(vmem_limit_bytes=48 << 20),
        name="weight_partial",
    )(core, *a, *b, *c)


def sum_kernel(y, parts, out):
    width = parts.shape[2]
    for b in range(NX):
        x = lax.rem(b - y[0] + NX, NX)
        total = parts[x].astype(F32)
        for z in range(1, NZ):
            total += parts[z * NX + x].astype(F32)
        out[:, b * width : (b + 1) * width] = total


def sum_parts(y, parts):
    sources, rows, width = parts.shape
    return pl.pallas_call(
        sum_kernel,
        grid_spec=pltpu.PrefetchScalarGridSpec(
            num_scalar_prefetch=1,
            grid=(1,),
            in_specs=[pl.BlockSpec((sources, rows, width), lambda i, y: (0, 0, 0))],
            out_specs=pl.BlockSpec((rows, NX * width), lambda i, y: (0, 0)),
        ),
        out_shape=jax.ShapeDtypeStruct((rows, NX * width), F32),
        cost_estimate=pl.CostEstimate(flops=sources * rows * width, bytes_accessed=2 << 20, transcendentals=0),
        name="sum_parts",
    )(y, parts)


def along_x(steps):
    return [(z * NX + x, z * NX + (x + steps) % NX) for z in range(NZ) for x in range(NX)]


def to_columns(steps):
    pairs = []
    for z in range(NZ):
        for x in range(NX):
            for y in range(NY):
                for c in range(2):
                    x_to = (x + steps) % NX
                    y_to = (y - x_to) % NY
                    pairs.append((((z * NX + x) * NY + y) * 2 + c, ((z * NX + x_to) * NY + y_to) * 2 + c))
    return pairs


def body(queries, key_rows, value_matrix, out_grad, inputs, doc_ids):
    shard = lax.axis_index("dp")
    tensor = lax.axis_index("tensor")
    tok = queries.shape[0]
    half = tok // 2
    shards = lax.axis_size("dp")
    first = shard * tok
    seg_own = lax.dynamic_slice_in_dim(doc_ids, first, tok)
    seg_prior = jnp.where(shard > 0, lax.dynamic_slice_in_dim(doc_ids, jnp.maximum(first - half, 0), half), -1)
    tail = jnp.concatenate([key_rows[half:], value_matrix[half:]], axis=1)
    prior = lax.ppermute(tail, "dp", [(i, i + 1) for i in range(shards - 1)])

    in_left = lax.ppermute(inputs, "dp", along_x(1))
    in_right = lax.ppermute(inputs, "dp", along_x(-1))
    in_far_low = lax.ppermute(in_left[:half], "dp", along_x(1))
    in_far_high = lax.ppermute(in_right[half:], "dp", along_x(-1))

    out_rows, query_grad, logsum, joined_low, back, dk_late, dv_late = attention(
        queries, out_grad, key_rows, value_matrix, prior, seg_own, seg_prior
    )
    back = lax.ppermute(back, "dp", [(i + 1, i) for i in range(shards - 1)])
    late = jnp.concatenate([dk_late[half:], dv_late[half:]], axis=1)
    joined_high = (late + back.astype(F32)).astype(BF16)
    joined = jnp.concatenate([joined_low, joined_high], axis=0)
    key_gradient = joined[:, :HEAD]
    value_gradient = joined[:, HEAD:]

    order = (0, 1, 3, 2)
    mine = [lax.ppermute(joined, ("dp", "tensor"), to_columns(d)) for d in order]
    swap = [(t, t ^ 1) for t in range(2 * NY)]
    other = [lax.ppermute(m, "tensor", swap) for m in mine]
    core = (tensor % 2).astype(jnp.int32).reshape(1)
    partial = weight_partial(core, (inputs, in_left, in_right, in_far_low, in_far_high), mine, other)
    parts = lax.all_to_all(partial, "dp", 0, 0, tiled=True)
    row = (tensor // 2).astype(jnp.int32).reshape(1)
    weight_grad = sum_parts(row, parts.reshape(shards, -1, 4 * HEAD))
    return out_rows, query_grad, key_gradient, value_gradient, logsum, weight_grad


def solution(mesh):
    split = P("dp", "tensor")
    return jax.shard_map(
        body,
        mesh=mesh,
        in_specs=(split, split, split, split, split, P()),
        out_specs=(split, split, split, split, P("tensor", "dp"), P(("tensor", "dp"), None)),
        check_vma=False,
    )
```

time: 412 us -> 132 us (0.32)
  waiting for transfers between devices: 252 us -> 61.3 us
  local copies, waits for them, and re-layouts: 62.2 us -> 12.2 us
  matrix products: 46.6 us -> 0 us
  starting transfers between devices: 11.4 us -> 36.5 us
  other arithmetic: 22.3 us -> 1.56 us
  Pallas kernels: 0 us -> 18.6 us
  between operations: 14.3 us -> 0.81 us
    unnamed x3 -> x0, waiting for transfers between devices: 214 us -> none
    dot_general x49 -> x0, matrix products: 46.6 us -> none  [the longest x8 12.9 us: attend_head(): jnp.einsum('rc,rd->cd', dscores, query_rows, preferred_element_type=jnp.f...]
    all_gather x1 -> x0, waiting for transfers between devices: 32.8 us -> none  [body(): kv_all = lax.all_gather(key_value_joined, 'tensor', axis=1, tiled=True)]
    ppermute x4 -> x14, waiting for transfers between devices: 4.91 us -> 35.1 us  [the longest x1 10.4 us: body(): prior = lax.ppermute(tail, 'dp', [(i, i + 1) for i in range(shards - 1)])]
    all_to_all x0 -> x1, waiting for transfers between devices: none -> 26.2 us  [body(): parts = lax.all_to_all(partial, 'dp', 0, 0, tiled=True)]
    pallas_call x0 -> x4, Pallas kernels: none -> 18.6 us  [the longest x1 5.55 us: weight_partial(): pl.pallas_call(weight_kernel, grid_spec=pltpu.PrefetchScalarGridSpec(num_...]
    dynamic_update_slice x16 -> x0, local copies, waits for them, and re-layouts: 16 us -> none  [kv_head(): sums, stacked = lax.scan(step, (empty, empty), (query_heads, grad_heads))]
    all_to_all x0 -> x1, starting transfers between devices: none -> 14.9 us  [body(): parts = lax.all_to_all(partial, 'dp', 0, 0, tiled=True)]
  transfers between devices with their start and end apart: 6 -> 15, of which waited for: 4 -> 10; matrix products, arithmetic and copies ran while one was open for 3% -> 6% of each run, Pallas kernels for 0% -> 8%
where the time goes in v1:
time: 132 us; the launch traced here: 131 us
  waiting for transfers between devices  61.3 us (46%)
  starting transfers between devices  36.5 us (28%)
  Pallas kernels  18.6 us (14%)
  local copies, waits for them, and re-layouts  12.2 us (9%)
  other arithmetic  1.56 us (1%)
    all_to_all x1, waiting for transfers between devices, body(): parts = lax.all_to_all(partial, 'dp', 0, 0, tiled=True)  26.2 us
    all_to_all x1, starting transfers between devices, body(): parts = lax.all_to_all(partial, 'dp', 0, 0, tiled=True)  14.9 us
    ppermute x4, starting transfers between devices, body(): lax.ppermute(joined, ('dp', 'tensor'), to_columns(d))  13.6 us
    ppermute x1, waiting for transfers between devices, body(): prior = lax.ppermute(tail, 'dp', [(i, i + 1) for i in range(shards - 1)])  10.4 us
    ppermute x4, waiting for transfers between devices, body(): lax.ppermute(joined, ('dp', 'tensor'), to_columns(d))  7.07 us
    ppermute x1, waiting for transfers between devices, body(): in_far_high = lax.ppermute(in_right[half:], 'dp', along_x(-1))  6.81 us
    unnamed x16, local copies, waits for them, and re-layouts  5.71 us
    pallas_call x1, Pallas kernels, weight_partial(): pl.pallas_call(weight_kernel, grid_spec=pltpu.PrefetchScalarGridSpec(num_...  5.55 us
  transfers between devices with their start and end apart: 15, of which 10 were waited for; matrix products, arithmetic and copies ran while one was open for 6% of the time, Pallas kernels for 8%

profile of v1, /device:TPU:2, one launch (start us, length us, event | category | flops | bytes accessed | tf_op | source)
XLA Modules:
  0.0 131.1 jit_solution(15941558843464037023)
XLA Ops:
  0.6 1.6 %collective-permute-start.2 = (bf16[512,1024]{1,0:T(8,128)(2,1)}, bf16[512,1024]{1,0:T(8,128)(2,1)}, u32[]{:S(2)}, u32[]{:S(2)}) collective-permute-start(bf16[512,1024]{1,0:T(8,128)(2,1)} %a0.1), channel_id=1, source_target_pairs={{0,8},{8,16},{16,24},{24,0},{32,40},{40,48},{48,56},{56,32},{64,72... | collective-permute-start | bytes 3145736 | tf_op jit(solution)/shard_map/ppermute | solution.py:220
  2.2 0.9 collective-permute-start.3
  3.1 0.8 slice.30
  3.9 0.8 slice.31
  4.8 3.1 %collective-permute-start = (bf16[256,256]{1,0:T(8,128)(2,1)S(1)}, bf16[256,256]{1,0:T(8,128)(2,1)S(1)}, u32[]{:S(2)}, u32[]{:S(2)}) collective-permute-start(bf16[256,256]{1,0:T(8,128)(2,1)S(1)} %pad_maximum_fusion.1), channel_id=1, source_target_pairs={{0,8},{8,16},{16,24},{24,32},{32,40},{40,48},{48,56},{56,64},{64,7... | collective-permute-start | bytes 393224 | tf_op jit(solution)/shard_map/ppermute | solution.py:218
  7.9 0.8 dynamic_slice.6
  8.6 0.8 dynamic-slice_select_fusion
  9.4 0.1 copy.19.sk
  9.6 0.1 copy.18.sk
  9.7 0.0 copy-start.1
  9.8 1.2 copy-done.1
  11.0 0.9 copy-done.2
  11.9 0.9 copy-done.3
  12.8 5.5 %attend_late.1 = (bf16[512,1024]{1,0:T(8,128)(2,1)}, bf16[512,1024]{1,0:T(8,128)(2,1)}, f32[8,512]{1,0:T(8,128)}, f32[512,128]{1,0:T(8,128)S(1)}, f32[512,128]{1,0:T(8,128)S(1)}) custom-call(bf16[512,1024]{1,0:T(8,128)(2,1)S(1)} %copy-done, bf16[512,1024]{1,0:T(8,128)(2,1)S(1)} %copy-done.1, bf16[512,128]{1,0:T(8,128)(2,1)S(1)} %copy-done.3, ...), custom_call_target="tpu_custom_call" | custom-call | flops 1207959552 | bytes 4194304 | tf_op jit(solution)/shard_map/attend_late/pallas_call | solution.py:106
  18.3 10.4 %collective-permute-done.k_lo.v_lo = bf16[256,256]{1,0:T(8,128)(2,1)S(1)} collective-permute-done((bf16[256,256]{1,0:T(8,128)(2,1)S(1)}, bf16[256,256]{1,0:T(8,128)(2,1)S(1)}, u32[]{:S(2)}, u32[]{:S(2)}) %collective-permute-start) | collective-permute-done | bytes 131104 | tf_op jit(solution)/shard_map/ppermute | solution.py:218
  28.6 5.5 %attend_early.1 = (bf16[512,1024]{1,0:T(8,128)(2,1)}, bf16[512,1024]{1,0:T(8,128)(2,1)}, f32[8,512]{1,0:T(8,128)}, bf16[256,256]{1,0:T(8,128)(2,1)S(1)}, bf16[256,256]{1,0:T(8,128)(2,1)S(1)}) custom-call(bf16[512,1024]{1,0:T(8,128)(2,1)S(1)} %copy-done, ...), custom_call_target="tpu_custom_call", output_to_operand_aliasing={{0}: (10, {}), {1}: (11, {}), {2}: (12, {})} | custom-call | flops 1207959552 | bytes 4194304 | tf_op jit(solution)/shard_map/attend_early/pallas_call | solution.py:120
  34.1 1.9 %collective-permute-start.1 = (bf16[256,256]{1,0:T(8,128)(2,1)S(1)}, bf16[256,256]{1,0:T(8,128)(2,1)S(1)}, u32[]{:S(2)}, u32[]{:S(2)}) collective-permute-start(bf16[256,256]{1,0:T(8,128)(2,1)S(1)} %get-tuple-element.24), channel_id=1, source_target_pairs={{8,0},{16,8},{24,16},{32,24},{40,32},{48,40},{56,48},{64,56},{72,6... | collective-permute-start | bytes 393224 | tf_op jit(solution)/shard_map/ppermute | solution.py:228
  36.1 4.9 %collective-permute-done.1 = bf16[256,256]{1,0:T(8,128)(2,1)S(1)} collective-permute-done((bf16[256,256]{1,0:T(8,128)(2,1)S(1)}, bf16[256,256]{1,0:T(8,128)(2,1)S(1)}, u32[]{:S(2)}, u32[]{:S(2)}) %collective-permute-start.1) | collective-permute-done | bytes 131104 | tf_op jit(solution)/shard_map/ppermute | solution.py:228
  41.0 0.0 copy-start.4
  41.1 4.2 %collective-permute-start.7 = (bf16[512,256]{1,0:T(8,128)(2,1)S(1)}, bf16[512,256]{1,0:T(8,128)(2,1)S(1)}, u32[]{:S(2)}, u32[]{:S(2)}) collective-permute-start(bf16[512,256]{1,0:T(8,128)(2,1)S(1)} %pad_maximum_fusion), channel_id=1, source_target_pairs={{0,14},{1,15},{2,8},{3,9},{4,10},{5,11},{6,12},{7,13},{8,20},{9,21... | collective-permute-start | bytes 786440 | tf_op jit(solution)/shard_map/ppermute | solution.py:236
  45.3 3.0 %collective-permute-start.6 = (bf16[512,256]{1,0:T(8,128)(2,1)S(1)}, bf16[512,256]{1,0:T(8,128)(2,1)S(1)}, u32[]{:S(2)}, u32[]{:S(2)}) collective-permute-start(bf16[512,256]{1,0:T(8,128)(2,1)S(1)} %pad_maximum_fusion), channel_id=1, source_target_pairs={{0,0},{1,1},{2,2},{3,3},{4,4},{5,5},{6,6},{7,7},{8,14},{9,15},{10,... | collective-permute-start | bytes 786440 | tf_op jit(solution)/shard_map/ppermute | solution.py:236
  48.2 0.3 collective-permute-start.8
  48.5 0.7 collective-permute-done.7.b1
  49.2 6.2 %collective-permute-start.9 = (bf16[512,256]{1,0:T(8,128)(2,1)S(1)}, bf16[512,256]{1,0:T(8,128)(2,1)S(1)}, u32[]{:S(2)}, u32[]{:S(2)}) collective-permute-start(bf16[512,256]{1,0:T(8,128)(2,1)S(1)} %pad_maximum_fusion), channel_id=1, source_target_pairs={{0,20},{1,21},{2,22},{3,23},{4,16},{5,17},{6,18},{7,19},{8,26},{9,... | collective-permute-start | bytes 786440 | tf_op jit(solution)/shard_map/ppermute | solution.py:236
  55.3 0.0 collective-permute-done.2.a1
  55.3 0.0 collective-permute-start.11
  55.3 1.9 %slice.44 = bf16[256,1024]{1,0:T(8,128)(2,1)} slice(bf16[512,1024]{1,0:T(8,128)(2,1)} %collective-permute-done.2.a1), slice={[0:256], [0:1024]} | slice | bytes 1048576 | tf_op jit(solution)/shard_map/slice | solution.py:222
  57.2 0.0 collective-permute-done.3.a3
  57.2 1.9 %slice.45 = bf16[256,1024]{1,0:T(8,128)(2,1)} slice(bf16[512,1024]{1,0:T(8,128)(2,1)} %collective-permute-done.3.a3), slice={[256:512], [0:1024]} | slice | bytes 1048576 | tf_op jit(solution)/shard_map/slice | solution.py:223
  59.1 6.4 %collective-permute-done.6.b0 = bf16[512,256]{1,0:T(8,128)(2,1)S(1)} collective-permute-done((bf16[512,256]{1,0:T(8,128)(2,1)S(1)}, bf16[512,256]{1,0:T(8,128)(2,1)S(1)}, u32[]{:S(2)}, u32[]{:S(2)}) %collective-permute-start.6) | collective-permute-done | bytes 262176 | tf_op jit(solution)/shard_map/ppermute | solution.py:236
  65.5 0.0 collective-permute-start.5
  65.5 0.0 collective-permute-done.9.b2
  65.5 0.5 collective-permute-start.12
  66.0 0.0 collective-permute-done.11.c1
  66.0 0.7 copy-done.5
  66.7 0.1 collective-permute-start.13
  66.8 0.3 collective-permute-done.10.c0
  67.2 0.4 collective-permute-done.12.c3
  67.6 0.8 collective-permute-done.13.c2
  68.4 4.4 %collective-permute-done.4.a2l = bf16[256,1024]{1,0:T(8,128)(2,1)S(1)} collective-permute-done((bf16[256,1024]{1,0:T(8,128)(2,1)}, bf16[256,1024]{1,0:T(8,128)(2,1)S(1)}, u32[]{:S(2)}, u32[]{:S(2)}) %collective-permute-start.4) | collective-permute-done | bytes 524320 | tf_op jit(solution)/shard_map/ppermute | solution.py:222
  72.8 6.8 %collective-permute-done.5.a2h = bf16[256,1024]{1,0:T(8,128)(2,1)S(1)} collective-permute-done((bf16[256,1024]{1,0:T(8,128)(2,1)}, bf16[256,1024]{1,0:T(8,128)(2,1)S(1)}, u32[]{:S(2)}, u32[]{:S(2)}) %collective-permute-start.5) | collective-permute-done | bytes 524320 | tf_op jit(solution)/shard_map/ppermute | solution.py:223
  79.6 0.9 copy-done.6
  80.5 5.6 %weight_partial.1 = bf16[1024,512]{1,0:T(8,128)(2,1)} custom-call(s32[1]{0:T(128)} %bitcast.5.core, bf16[512,1024]{1,0:T(8,128)(2,1)S(1)} %copy-done.4, bf16[512,1024]{1,0:T(8,128)(2,1)} %collective-permute-done.2.a1, bf16[512,1024]{1,0:T(8,128)(2,1)} %collective-permute-done.3.a3, bf16[256,1024]{1,0:T(8,128)(2,1)S(1)} %collective-permute-done.4.a2l, ...), custom_call_target="tpu_custom_call" | custom-call | flops 2147483648 | bytes 8388608 | tf_op jit(solution)/shard_map/weight_partial/pallas_call | solution.py:151
  86.1 14.9 %all-to-all-start = ((bf16[32,32,512]{2,1,0:T(8,128)(2,1)}), bf16[32,32,512]{2,1,0:T(8,128)(2,1)S(1)}, u32[]{:S(2)}, u32[]{:S(2)}) async-start(bf16[32,32,512]{2,1,0:T(8,128)(2,1)} %bitcast.6), calls=%async_computation | async-start | bytes 2097152 | tf_op jit(solution)/shard_map/all_to_all | solution.py:241
  101.0 0.7 fusion.2
  101.7 26.2 %all-to-all-done.parts = bf16[32,32,512]{2,1,0:T(8,128)(2,1)S(1)} async-done(((bf16[32,32,512]{2,1,0:T(8,128)(2,1)}), bf16[32,32,512]{2,1,0:T(8,128)(2,1)S(1)}, u32[]{:S(2)}, u32[]{:S(2)}) %all-to-all-start) | async-done | bytes 1048608 | tf_op jit(solution)/shard_map/all_to_all | solution.py:241
  128.0 1.0 copy-done.7
  129.0 2.1 %sum_parts.1 = f32[32,2048]{1,0:T(8,128)} custom-call(s32[1]{0:T(128)} %bitcast.4.y, bf16[32,32,512]{2,1,0:T(8,128)(2,1)} %copy-done.7), custom_call_target="tpu_custom_call" | custom-call | flops 524288 | bytes 2097152 | tf_op jit(solution)/shard_map/sum_parts/pallas_call | solution.py:178
  (18 shorter events, 0.1 us)
Async XLA Ops:
  0.6 9.1 %copy-start = (bf16[512,1024]{1,0:T(8,128)(2,1)S(1)}, bf16[512,1024]{1,0:T(8,128)(2,1)}, u32[]{:S(2)}) copy-start(bf16[512,1024]{1,0:T(8,128)(2,1)} %q.3) | copy-start | bytes 3145732
  0.6 54.7 %collective-permute-start.2 = (bf16[512,1024]{1,0:T(8,128)(2,1)}, bf16[512,1024]{1,0:T(8,128)(2,1)}, u32[]{:S(2)}, u32[]{:S(2)}) collective-permute-start(bf16[512,1024]{1,0:T(8,128)(2,1)} %a0.1), channel_id=1, source_target_pairs={{0,8},{8,16},{16,24},{24,0},{32,40},{40,48},{48,56},{56,32},{64,72... | collective-permute-start | bytes 3145736 | tf_op jit(solution)/shard_map/ppermute | solution.py:220
  2.2 55.0 %collective-permute-start.3 = (bf16[512,1024]{1,0:T(8,128)(2,1)}, bf16[512,1024]{1,0:T(8,128)(2,1)}, u32[]{:S(2)}, u32[]{:S(2)}) collective-permute-start(bf16[512,1024]{1,0:T(8,128)(2,1)} %a0.1), channel_id=1, source_target_pairs={{0,24},{8,0},{16,8},{24,16},{32,56},{40,32},{48,40},{56,48},{64,88... | collective-permute-start | bytes 3145736 | tf_op jit(solution)/shard_map/ppermute | solution.py:221
  4.8 23.8 %collective-permute-start = (bf16[256,256]{1,0:T(8,128)(2,1)S(1)}, bf16[256,256]{1,0:T(8,128)(2,1)S(1)}, u32[]{:S(2)}, u32[]{:S(2)}) collective-permute-start(bf16[256,256]{1,0:T(8,128)(2,1)S(1)} %pad_maximum_fusion.1), channel_id=1, source_target_pairs={{0,8},{8,16},{16,24},{24,32},{32,40},{40,48},{48,56},{56,64},{64,7... | collective-permute-start | bytes 393224 | tf_op jit(solution)/shard_map/ppermute | solution.py:218
  9.7 1.2 copy-start.1
  11.0 0.9 copy-start.2
  11.9 0.9 copy-start.3
  34.1 6.8 %collective-permute-start.1 = (bf16[256,256]{1,0:T(8,128)(2,1)S(1)}, bf16[256,256]{1,0:T(8,128)(2,1)S(1)}, u32[]{:S(2)}, u32[]{:S(2)}) collective-permute-start(bf16[256,256]{1,0:T(8,128)(2,1)S(1)} %get-tuple-element.24), channel_id=1, source_target_pairs={{8,0},{16,8},{24,16},{32,24},{40,32},{48,40},{56,48},{64,56},{72,6... | collective-permute-start | bytes 393224 | tf_op jit(solution)/shard_map/ppermute | solution.py:228
  41.0 38.5 %copy-start.4 = (bf16[512,1024]{1,0:T(8,128)(2,1)S(1)}, bf16[512,1024]{1,0:T(8,128)(2,1)}, u32[]{:S(2)}) copy-start(bf16[512,1024]{1,0:T(8,128)(2,1)} %a0.1) | copy-start | bytes 3145732
  41.1 8.1 %collective-permute-start.7 = (bf16[512,256]{1,0:T(8,128)(2,1)S(1)}, bf16[512,256]{1,0:T(8,128)(2,1)S(1)}, u32[]{:S(2)}, u32[]{:S(2)}) collective-permute-start(bf16[512,256]{1,0:T(8,128)(2,1)S(1)} %pad_maximum_fusion), channel_id=1, source_target_pairs={{0,14},{1,15},{2,8},{3,9},{4,10},{5,11},{6,12},{7,13},{8,20},{9,21... | collective-permute-start | bytes 786440 | tf_op jit(solution)/shard_map/ppermute | solution.py:236
  45.3 20.2 %collective-permute-start.6 = (bf16[512,256]{1,0:T(8,128)(2,1)S(1)}, bf16[512,256]{1,0:T(8,128)(2,1)S(1)}, u32[]{:S(2)}, u32[]{:S(2)}) collective-permute-start(bf16[512,256]{1,0:T(8,128)(2,1)S(1)} %pad_maximum_fusion), channel_id=1, source_target_pairs={{0,0},{1,1},{2,2},{3,3},{4,4},{5,5},{6,6},{7,7},{8,14},{9,15},{10,... | collective-permute-start | bytes 786440 | tf_op jit(solution)/shard_map/ppermute | solution.py:236
  48.2 17.3 %collective-permute-start.8 = (bf16[512,256]{1,0:T(8,128)(2,1)S(1)}, bf16[512,256]{1,0:T(8,128)(2,1)S(1)}, u32[]{:S(2)}, u32[]{:S(2)}) collective-permute-start(bf16[512,256]{1,0:T(8,128)(2,1)S(1)} %pad_maximum_fusion), channel_id=1, source_target_pairs={{0,26},{1,27},{2,28},{3,29},{4,30},{5,31},{6,24},{7,25},{8,0},{9,1... | collective-permute-start | bytes 786440 | tf_op jit(solution)/shard_map/ppermute | solution.py:236
  49.2 16.4 %collective-permute-start.9 = (bf16[512,256]{1,0:T(8,128)(2,1)S(1)}, bf16[512,256]{1,0:T(8,128)(2,1)S(1)}, u32[]{:S(2)}, u32[]{:S(2)}) collective-permute-start(bf16[512,256]{1,0:T(8,128)(2,1)S(1)} %pad_maximum_fusion), channel_id=1, source_target_pairs={{0,20},{1,21},{2,22},{3,23},{4,16},{5,17},{6,18},{7,19},{8,26},{9,... | collective-permute-start | bytes 786440 | tf_op jit(solution)/shard_map/ppermute | solution.py:236
  55.3 10.7 %collective-permute-start.11 = (bf16[512,256]{1,0:T(8,128)(2,1)S(1)}, bf16[512,256]{1,0:T(8,128)(2,1)S(1)}, u32[]{:S(2)}, u32[]{:S(2)}) collective-permute-start(bf16[512,256]{1,0:T(8,128)(2,1)S(1)} %collective-permute-done.7.b1), channel_id=1, source_target_pairs={{0,1},{1,0},{2,3},{3,2},{4,5},{5,4},{6,7},{7,6},{8,9},{9,8},{10,11... | collective-permute-start | bytes 786440 | tf_op jit(solution)/shard_map/ppermute | solution.py:238
  57.2 15.6 %collective-permute-start.4 = (bf16[256,1024]{1,0:T(8,128)(2,1)}, bf16[256,1024]{1,0:T(8,128)(2,1)S(1)}, u32[]{:S(2)}, u32[]{:S(2)}) collective-permute-start(bf16[256,1024]{1,0:T(8,128)(2,1)} %slice.44), channel_id=1, source_target_pairs={{0,8},{8,16},{16,24},{24,0},{32,40},{40,48},{48,56},{56,32},{64,72... | collective-permute-start | bytes 1572872 | tf_op jit(solution)/shard_map/ppermute | solution.py:222
  65.5 14.1 %collective-permute-start.5 = (bf16[256,1024]{1,0:T(8,128)(2,1)}, bf16[256,1024]{1,0:T(8,128)(2,1)S(1)}, u32[]{:S(2)}, u32[]{:S(2)}) collective-permute-start(bf16[256,1024]{1,0:T(8,128)(2,1)} %slice.45), channel_id=1, source_target_pairs={{0,24},{8,0},{16,8},{24,16},{32,56},{40,32},{48,40},{56,48},{64,88... | collective-permute-start | bytes 1572872 | tf_op jit(solution)/shard_map/ppermute | solution.py:223
  65.5 1.7 %collective-permute-start.10 = (bf16[512,256]{1,0:T(8,128)(2,1)S(1)}, bf16[512,256]{1,0:T(8,128)(2,1)}, u32[]{:S(2)}, u32[]{:S(2)}) collective-permute-start(bf16[512,256]{1,0:T(8,128)(2,1)S(1)} %collective-permute-done.6.b0), channel_id=1, source_target_pairs={{0,1},{1,0},{2,3},{3,2},{4,5},{5,4},{6,7},{7,6},{8,9},{9,8},{10,11... | collective-permute-start | bytes 786440 | tf_op jit(solution)/shard_map/ppermute | solution.py:238
  65.5 2.0 %collective-permute-start.12 = (bf16[512,256]{1,0:T(8,128)(2,1)S(1)}, bf16[512,256]{1,0:T(8,128)(2,1)}, u32[]{:S(2)}, u32[]{:S(2)}) collective-permute-start(bf16[512,256]{1,0:T(8,128)(2,1)S(1)} %collective-permute-done.8.b3), channel_id=1, source_target_pairs={{0,1},{1,0},{2,3},{3,2},{4,5},{5,4},{6,7},{7,6},{8,9},{9,8},{10,11... | collective-permute-start | bytes 786440 | tf_op jit(solution)/shard_map/ppermute | solution.py:238
  66.0 0.7 copy-start.5
  66.7 1.7 %collective-permute-start.13 = (bf16[512,256]{1,0:T(8,128)(2,1)S(1)}, bf16[512,256]{1,0:T(8,128)(2,1)}, u32[]{:S(2)}, u32[]{:S(2)}) collective-permute-start(bf16[512,256]{1,0:T(8,128)(2,1)S(1)} %collective-permute-done.9.b2), channel_id=1, source_target_pairs={{0,1},{1,0},{2,3},{3,2},{4,5},{5,4},{6,7},{7,6},{8,9},{9,8},{10,11... | collective-permute-start | bytes 786440 | tf_op jit(solution)/shard_map/ppermute | solution.py:238
  79.6 1.0 copy-start.6
  86.1 41.9 %all-to-all-start = ((bf16[32,32,512]{2,1,0:T(8,128)(2,1)}), bf16[32,32,512]{2,1,0:T(8,128)(2,1)S(1)}, u32[]{:S(2)}, u32[]{:S(2)}) async-start(bf16[32,32,512]{2,1,0:T(8,128)(2,1)} %bitcast.6), calls=%async_computation | async-start | bytes 2097152 | tf_op jit(solution)/shard_map/all_to_all | solution.py:241
  128.0 1.0 copy-start.7

commit v2 on v1

v2 whole, which is shorter than its diff:
```python
import jax
import jax.numpy as jnp
from jax import lax
from jax.experimental import pallas as pl
from jax.experimental.pallas import tpu as pltpu
from jax.sharding import PartitionSpec as P

HEAD = 128
REACH = 256
BLOCK = 128
WINDOW = REACH + BLOCK
NX, NY, NZ = 4, 4, 8
ORDER = (0, 1, 3, 2)
F32 = jnp.float32
BF16 = jnp.bfloat16
NT = (((1,), (1,)), ((), ()))
TN = (((0,), (0,)), ((), ()))


def dot(a, b, dims=(((1,), (0,)), ((), ()))):
    return lax.dot_general(a, b, dims, preferred_element_type=F32)


def attend_rows(q_ref, g_ref, k_lo, k_hi, v_lo, v_hi, doc_ref, first, o_ref, dq_ref, lse_ref, dk_ref, dv_ref, p_s, ds_s):
    heads = q_ref.shape[1] // HEAD
    scale = HEAD ** (-0.5)
    keys = jnp.concatenate([k_lo[...], k_hi[...]], axis=0)
    vals = jnp.concatenate([v_lo[...], v_hi[...]], axis=0)
    docs = [doc_ref[pl.ds(jnp.maximum(first + b, 0), 1), :].astype(F32) for b in range((2 * REACH) // BLOCK)]
    docs = [jnp.broadcast_to(jnp.where(first + b >= 0, d, -1.0), (BLOCK, BLOCK)) for b, d in enumerate(docs)]
    docs_t = [d.T for d in docs]
    keys_t = keys.T
    vals_t = vals.T
    dk_ref[...] = jnp.zeros_like(dk_ref)
    dv_ref[...] = jnp.zeros_like(dv_ref)
    for j in range(REACH // BLOCK):
        lo = j * BLOCK
        rows = slice(lo, lo + BLOCK)
        win = slice(lo, lo + WINDOW)
        k_w, v_w = keys[win], vals[win]
        kt_w, vt_w = keys_t[:, win], vals_t[:, win]
        key_at = lax.broadcasted_iota(jnp.int32, (WINDOW, BLOCK), 0)
        query_at = lax.broadcasted_iota(jnp.int32, (WINDOW, BLOCK), 1) + REACH
        own = docs[j + REACH // BLOCK]
        same = jnp.concatenate([jnp.where(d == own, 1.0, 0.0) for d in docs_t[j : j + WINDOW // BLOCK]], axis=0)
        allowed = (same > 0.5) & (key_at <= query_at)
        bias = jnp.where(allowed, 0.0, -1e30).astype(F32)
        bias = jnp.concatenate([bias, bias], axis=1)
        q_parts, g_parts = [], []
        for h in range(0, heads, 2):
            c0 = slice(h * HEAD, (h + 1) * HEAD)
            c1 = slice((h + 1) * HEAD, (h + 2) * HEAD)
            qp = jnp.concatenate([q_ref[rows, c0], q_ref[rows, c1]], axis=0)
            gp = jnp.concatenate([g_ref[rows, c0], g_ref[rows, c1]], axis=0)
            q_parts.append(qp)
            g_parts.append(gp)
            s = dot(k_w, qp, NT) * scale + bias
            top = jnp.max(s, axis=0, keepdims=True)
            e = jnp.exp(s - top)
            total = jnp.sum(e, axis=0, keepdims=True)
            lse = top + jnp.log(total)
            lse_ref[h : h + 1, rows] = lse[:, :BLOCK]
            lse_ref[h + 1 : h + 2, rows] = lse[:, BLOCK:]
            p = e * (1.0 / total)
            dp = dot(v_w, gp, NT)
            delta = jnp.sum(p * dp, axis=0, keepdims=True)
            ds = (p * (dp - delta)).astype(BF16)
            p_low = p.astype(BF16)
            cols = slice(h * BLOCK, (h + 2) * BLOCK)
            p_s[:, cols] = p_low
            ds_s[:, cols] = ds
            o = dot(vt_w, p_low).T
            o_ref[rows, c0] = o[:BLOCK].astype(BF16)
            o_ref[rows, c1] = o[BLOCK:].astype(BF16)
            dq = (dot(kt_w, ds) * scale).T
            dq_ref[rows, c0] = dq[:BLOCK].astype(BF16)
            dq_ref[rows, c1] = dq[BLOCK:].astype(BF16)
        dv_ref[win, :] += dot(p_s[...], jnp.concatenate(g_parts, axis=0))
        dk_ref[win, :] += dot(ds_s[...], jnp.concatenate(q_parts, axis=0)) * scale


def early_kernel(q, g, k_lo, k_hi, v_lo, v_hi, doc, o, dq, lse, dk_own, dv_own, back, p_s, ds_s, dk, dv):
    first = lax.axis_index("dp") * (2 * REACH // BLOCK) - REACH // BLOCK
    attend_rows(q, g, k_lo, k_hi, v_lo, v_hi, doc, first, o, dq, lse, dk, dv, p_s, ds_s)
    back[:, :HEAD] = dk[:REACH].astype(BF16)
    back[:, HEAD:] = dv[:REACH].astype(BF16)
    dk_own[...] = dk[REACH:]
    dv_own[...] = dv[REACH:]


def late_kernel(q, g, k_lo, k_hi, v_lo, v_hi, doc, dk_own, dv_own, o_in, dq_in, lse_in, o, dq, lse, low, high, p_s, ds_s, dk, dv):
    first = lax.axis_index("dp") * (2 * REACH // BLOCK)
    attend_rows(q, g, k_lo, k_hi, v_lo, v_hi, doc, first, o, dq, lse, dk, dv, p_s, ds_s)
    low[:, :HEAD] = (dk[:REACH] + dk_own[...]).astype(BF16)
    low[:, HEAD:] = (dv[:REACH] + dv_own[...]).astype(BF16)
    high[:, :HEAD] = dk[REACH:]
    high[:, HEAD:] = dv[REACH:]


def spec(shape, at):
    return pl.BlockSpec(shape, lambda i: at)


def attention(queries, out_grad, key_rows, value_matrix, prior_keys, prior_vals, docs):
    tok, width = queries.shape
    heads = width // HEAD
    half = tok // 2
    cost = pl.CostEstimate(flops=6 * 2 * half * WINDOW * width, bytes_accessed=32 << 20, transcendentals=half * WINDOW * heads)
    params = pltpu.CompilerParams(vmem_limit_bytes=60 << 20)
    wide = lambda i: spec((half, width), (i, 0))
    kv = lambda i: spec((half, HEAD), (i, 0))
    doc = spec(docs.shape, (0, 0))
    scratch = [pltpu.VMEM((WINDOW, heads * BLOCK), BF16)] * 2 + [pltpu.VMEM((tok, HEAD), F32)] * 2
    rows_out = jax.ShapeDtypeStruct((tok, width), BF16)
    lse_out = jax.ShapeDtypeStruct((heads, tok), F32)
    grad = jax.ShapeDtypeStruct((half, HEAD), F32)
    part = spec((half, HEAD), (0, 0))
    pair = spec((half, 2 * HEAD), (0, 0))
    o, dq, lse, dk_own, dv_own, back = pl.pallas_call(
        early_kernel,
        grid=(1,),
        in_specs=[wide(0), wide(0), kv(1), kv(0), kv(1), kv(0), doc],
        out_specs=[wide(0), wide(0), spec((heads, half), (0, 0)), part, part, pair],
        out_shape=[rows_out, rows_out, lse_out, grad, grad, jax.ShapeDtypeStruct((half, 2 * HEAD), BF16)],
        scratch_shapes=scratch,
        cost_estimate=cost,
        compiler_params=params,
        name="attend_early",
    )(queries, out_grad, prior_keys, key_rows, prior_vals, value_matrix, docs)
    hbm = pl.BlockSpec(memory_space=pl.ANY)
    o, dq, lse, low, high = pl.pallas_call(
        late_kernel,
        grid=(1,),
        in_specs=[wide(1), wide(1), kv(0), kv(1), kv(0), kv(1), doc, part, part, hbm, hbm, hbm],
        out_specs=[wide(1), wide(1), spec((heads, half), (0, 1)), pair, pair],
        out_shape=[rows_out, rows_out, lse_out, jax.ShapeDtypeStruct((half, 2 * HEAD), BF16), jax.ShapeDtypeStruct((half, 2 * HEAD), F32)],
        scratch_shapes=scratch,
        input_output_aliases={9: 0, 10: 1, 11: 2},
        cost_estimate=cost,
        compiler_params=params,
        name="attend_late",
    )(queries, out_grad, key_rows, key_rows, value_matrix, value_matrix, docs, dk_own, dv_own, o, dq, lse)
    return o, dq, lse, back, low, high, dk_own


def split_kernel(x, first, second):
    half = first.shape[1]
    first[...] = x[:, :half]
    second[...] = x[:, half:]


def split_inputs(inputs):
    tok, width = inputs.shape
    part = jax.ShapeDtypeStruct((tok, width // 2), BF16)
    return pl.pallas_call(
        split_kernel,
        grid=(1,),
        in_specs=[spec((tok, width), (0, 0))],
        out_specs=[spec((tok, width // 2), (0, 0))] * 2,
        out_shape=[part, part],
        compiler_params=pltpu.CompilerParams(vmem_limit_bytes=48 << 20),
        name="split_inputs",
    )(inputs)


def join_kernel(low, high, back, joined, key_grad, value_grad):
    half = low.shape[0]
    rest = (high[...] + back[...].astype(F32)).astype(BF16)
    joined[:half] = low[...]
    joined[half:] = rest
    key_grad[:half] = low[:, :HEAD]
    key_grad[half:] = rest[:, :HEAD]
    value_grad[:half] = low[:, HEAD:]
    value_grad[half:] = rest[:, HEAD:]


def join_gradients(low, high, back):
    half, width = low.shape
    part = spec((half, width), (0, 0))
    shapes = [(2 * half, width), (2 * half, HEAD), (2 * half, HEAD)]
    return pl.pallas_call(
        join_kernel,
        grid=(1,),
        in_specs=[part] * 3,
        out_specs=[spec(shape, (0, 0)) for shape in shapes],
        out_shape=[jax.ShapeDtypeStruct(shape, BF16) for shape in shapes],
        name="join_gradients",
    )(low, high, back)


def weight_kernel(a0, a1, a3, a2, d0, d1, d3, d2, b0, b1, b3, b2, c0, c1, c3, c2, out):
    core = lax.rem(lax.axis_index("tensor"), 2)
    mine = pl.ds(pl.multiple_of(core * 2 * HEAD, 2 * HEAD), 2 * HEAD)
    other = pl.ds(pl.multiple_of((1 - core) * 2 * HEAD, 2 * HEAD), 2 * HEAD)

    def multiply(left):
        for cols, right in ((mine, (b0, b1, b3, b2)), (other, (c0, c1, c3, c2))):
            total = dot(left[0][...], right[0][...], TN)
            for l, r in zip(left[1:], right[1:]):
                total += dot(l[...], r[...], TN)
            out[:, cols] = total.astype(BF16)

    steps = pl.num_programs(0) // 2

    @pl.when(pl.program_id(0) < steps)
    def _():
        multiply((a0, a1, a3, a2))

    @pl.when(pl.program_id(0) >= steps)
    def _():
        multiply((d0, d1, d3, d2))


def weight_partial(first, second, mine, other):
    tile = 2 * HEAD
    tok, width = first[0].shape
    steps = width // tile
    low = pl.BlockSpec((tok, tile), lambda i: (0, jnp.minimum(i, steps - 1)))
    high = pl.BlockSpec((tok, tile), lambda i: (0, jnp.maximum(i - steps, 0)))
    whole = pl.BlockSpec((tok, 2 * HEAD), lambda i: (0, 0))
    return pl.pallas_call(
        weight_kernel,
        grid=(2 * steps,),
        in_specs=[low] * 4 + [high] * 4 + [whole] * 8,
        out_specs=pl.BlockSpec((tile, 4 * HEAD), lambda i: (i, 0)),
        out_shape=jax.ShapeDtypeStruct((2 * width, 4 * HEAD), BF16),
        cost_estimate=pl.CostEstimate(flops=4 * width * 4 * HEAD * 4 * tok, bytes_accessed=8 << 20, transcendentals=0),
        compiler_params=pltpu.CompilerParams(vmem_limit_bytes=60 << 20),
        name="weight_partial",
    )(*first, *second, *mine, *other)


def sum_kernel(parts, out):
    y = lax.axis_index("tensor") // 2
    wide = 2 * HEAD
    for head in range(2 * NX):
        x = lax.rem(head // 2 - y + NX + 2 * (head % 2), NX)
        side = slice((head % 2) * wide, (head % 2 + 1) * wide)
        total = parts[x, :, side].astype(F32)
        for z in range(1, NZ):
            total += parts[z * NX + x, :, side].astype(F32)
        out[:, head * wide : (head + 1) * wide] = total


def sum_parts(parts):
    sources, rows, width = parts.shape
    return pl.pallas_call(
        sum_kernel,
        grid=(1,),
        in_specs=[spec((sources, rows, width), (0, 0, 0))],
        out_specs=spec((rows, NX * width), (0, 0)),
        out_shape=jax.ShapeDtypeStruct((rows, NX * width), F32),
        cost_estimate=pl.CostEstimate(flops=sources * rows * width, bytes_accessed=2 << 20, transcendentals=0),
        compiler_params=pltpu.CompilerParams(vmem_limit_bytes=60 << 20),
        name="sum_parts",
    )(parts)


def along_x(steps):
    return [(z * NX + x, z * NX + (x + steps) % NX) for z in range(NZ) for x in range(NX)]


def to_columns(steps):
    pairs = []
    for z in range(NZ):
        for x in range(NX):
            for y in range(NY):
                for c in range(2):
                    x_to = (x + steps) % NX
                    y_to = (y - x_to - 2 * c) % NY
                    pairs.append((((z * NX + x) * NY + y) * 2 + c, ((z * NX + x_to) * NY + y_to) * 2 + c))
    return pairs


def after(value, *others):
    return lax.optimization_barrier((value, *others))[0]


def body(queries, key_rows, value_matrix, out_grad, inputs, doc_ids):
    shards = lax.axis_size("dp")
    docs = doc_ids.reshape(-1, BLOCK)
    onward = [(i, i + 1) for i in range(shards - 1)]
    backward = [(i + 1, i) for i in range(shards - 1)]
    prior_keys = lax.ppermute(key_rows, "dp", onward)
    prior_vals = lax.ppermute(value_matrix, "dp", onward)

    first, second = split_inputs(inputs)
    first_sent = after(first, prior_keys, prior_vals)
    first_left = lax.ppermute(first_sent, "dp", along_x(1))
    first_right = lax.ppermute(first_sent, "dp", along_x(-1))

    out_rows, query_grad, logsum, back, low, high, dk_early = attention(
        queries, out_grad, key_rows, value_matrix, prior_keys, prior_vals, docs
    )
    second_left = lax.ppermute(after(second, dk_early), "dp", along_x(1))
    back = lax.ppermute(back, "dp", backward)
    second_right = lax.ppermute(after(second, back), "dp", along_x(-1))
    first_far = lax.ppermute(after(first_left, low), "dp", along_x(1))
    second_far = lax.ppermute(second_right, "dp", along_x(-1))
    joined, key_gradient, value_gradient = join_gradients(low, high, after(back, first_right, first_left))

    mine = [lax.ppermute(joined, ("dp", "tensor"), to_columns(d)) for d in ORDER]
    swap = [(t, t ^ 1) for t in range(2 * NY)]
    other = [lax.ppermute(m, "tensor", swap) for m in mine]
    first_all = (first, first_left, first_right, first_far)
    second_all = (second, second_left, second_right, second_far)
    partial = weight_partial(first_all, second_all, mine, other)
    parts = lax.all_to_all(partial, "dp", 0, 0, tiled=True)
    weight_grad = sum_parts(parts.reshape(shards, -1, 4 * HEAD))
    return out_rows, query_grad, key_gradient, value_gradient, logsum, weight_grad


def solution(mesh):
    split = P("dp", "tensor")
    return jax.shard_map(
        body,
        mesh=mesh,
        in_specs=(split, split, split, split, split, P()),
        out_specs=(split, split, split, split, P("tensor", "dp"), P(("tensor", "dp"), None)),
        check_vma=False,
    )
```

time: 132 us -> 118 us (0.89)
  waiting for transfers between devices: 61.3 us -> 13.9 us
  blocking collectives: 0 us -> 38 us
  local copies, waits for them, and re-layouts: 12.2 us -> 3.14 us
  Pallas kernels: 18.6 us -> 24.5 us
  other arithmetic: 1.56 us -> 0 us
    all_to_all x0 -> x1, blocking collectives: none -> 38 us  [body(): parts = lax.all_to_all(partial, 'dp', 0, 0, tiled=True)]
    all_to_all x1 -> x0, waiting for transfers between devices: 26.2 us -> none  [body(): parts = lax.all_to_all(partial, 'dp', 0, 0, tiled=True)]
    ppermute x6 -> x9, waiting for transfers between devices: 26.4 us -> 10 us  [the longest x1 4.27 us: body(): second_far = lax.ppermute(second_right, 'dp', along_x(-1))]
    all_to_all x1 -> x0, starting transfers between devices: 14.9 us -> none  [body(): parts = lax.all_to_all(partial, 'dp', 0, 0, tiled=True)]
    ppermute x6 -> x9, starting transfers between devices: 7.42 us -> 21.2 us  [the longest x1 6.36 us: body(): second_far = lax.ppermute(second_right, 'dp', along_x(-1))]
    slice x7 -> x0, local copies, waits for them, and re-layouts: 5.47 us -> none  [the longest x1 1.88 us: body(): in_far_low = lax.ppermute(in_left[:half], 'dp', along_x(1))]
    ppermute x4, waiting for transfers between devices: 7.07 us -> 2.23 us  [body(): lax.ppermute(joined, ('dp', 'tensor'), to_columns(d))]
    pallas_call x3 -> x5, Pallas kernels: 13.1 us -> 17.5 us  [the longest x1 6.87 us: attention(): pl.pallas_call(early_kernel, grid=(1,), in_specs=[wide(0), wide(0), kv(1)...]
  transfers between devices with their start and end apart: 15 -> 17, of which waited for: 10 -> 7; matrix products, arithmetic and copies ran while one was open for 6% -> 0% of each run, Pallas kernels for 8% -> 13%
where the time goes in v2:
time: 118 us; the launch traced here: 117 us
  blocking collectives  38 us (32%)
  starting transfers between devices  36.7 us (31%)
  Pallas kernels  24.5 us (21%)
  waiting for transfers between devices  13.9 us (12%)
  local copies, waits for them, and re-layouts  3.14 us (3%)
    all_to_all x1, blocking collectives, body(): parts = lax.all_to_all(partial, 'dp', 0, 0, tiled=True)  38 us
    ppermute x4, starting transfers between devices, body(): lax.ppermute(joined, ('dp', 'tensor'), to_columns(d))  14.9 us
    pallas_call x1, Pallas kernels, attention(): pl.pallas_call(late_kernel, grid=(1,), in_specs=[wide(1), wide(1), kv(0),...  6.99 us
    pallas_call x1, Pallas kernels, attention(): pl.pallas_call(early_kernel, grid=(1,), in_specs=[wide(0), wide(0), kv(1)...  6.87 us
    pallas_call x1, Pallas kernels, weight_partial(): pl.pallas_call(weight_kernel, grid=(2 * steps,), in_specs=[low] * 4 + [hi...  6.65 us
    ppermute x1, starting transfers between devices, body(): second_far = lax.ppermute(second_right, 'dp', along_x(-1))  6.36 us
    ppermute x1, waiting for transfers between devices, body(): second_far = lax.ppermute(second_right, 'dp', along_x(-1))  4.27 us
    ppermute x1, starting transfers between devices, body(): back = lax.ppermute(back, 'dp', backward)  3.51 us
  transfers between devices with their start and end apart: 17, of which 7 were waited for; matrix products, arithmetic and copies ran while one was open for 0% of the time, Pallas kernels for 13%

profile of v2, /device:TPU:2, one launch (start us, length us, event | category | flops | bytes accessed | tf_op | source)
XLA Modules:
  0.0 117.1 jit_solution(588267739287894413)
XLA Ops:
  0.6 3.4 %collective-permute-start = (bf16[512,128]{1,0:T(8,128)(2,1)}, bf16[512,128]{1,0:T(8,128)(2,1)S(1)}, u32[]{:S(2)}, u32[]{:S(2)}) collective-permute-start(bf16[512,128]{1,0:T(8,128)(2,1)} %k_hi.3), channel_id=1, source_target_pairs={{0,8},{8,16},{16,24},{24,32},{32,40},{40,48},{48,56},{56,64},{64,7... | collective-permute-start | bytes 393224 | tf_op jit(solution)/shard_map/ppermute | solution.py:284
  4.0 3.1 %collective-permute-start.1 = (bf16[512,128]{1,0:T(8,128)(2,1)}, bf16[512,128]{1,0:T(8,128)(2,1)S(1)}, u32[]{:S(2)}, u32[]{:S(2)}) collective-permute-start(bf16[512,128]{1,0:T(8,128)(2,1)} %v_hi.3), channel_id=1, source_target_pairs={{0,8},{8,16},{16,24},{24,32},{32,40},{40,48},{48,56},{56,64},{64,7... | collective-permute-start | bytes 393224 | tf_op jit(solution)/shard_map/ppermute | solution.py:285
  7.2 0.0 copy-start
  7.2 1.2 %copy-done = bf16[512,1024]{1,0:T(8,128)(2,1)S(1)} copy-done((bf16[512,1024]{1,0:T(8,128)(2,1)S(1)}, bf16[512,1024]{1,0:T(8,128)(2,1)}, u32[]{:S(2)}) %copy-start) | copy-done | bytes 1048600
  8.4 0.1 split_inputs.1
  8.5 0.0 collective-permute-done.k_lo
  8.5 0.0 copy-start.18
  8.5 2.6 %collective-permute-done.1.v_lo = bf16[512,128]{1,0:T(8,128)(2,1)S(1)} collective-permute-done((bf16[512,128]{1,0:T(8,128)(2,1)}, bf16[512,128]{1,0:T(8,128)(2,1)S(1)}, u32[]{:S(2)}, u32[]{:S(2)}) %collective-permute-start.1) | collective-permute-done | bytes 131104 | tf_op jit(solution)/shard_map/ppermute | solution.py:285
  11.1 1.2 %collective-permute-start.4 = (bf16[512,512]{1,0:T(8,128)(2,1)S(1)}, bf16[512,512]{1,0:T(8,128)(2,1)S(1)}, u32[]{:S(2)}, u32[]{:S(2)}) collective-permute-start(bf16[512,512]{1,0:T(8,128)(2,1)S(1)} %get-tuple-element.38.a0), channel_id=1, source_target_pairs={{0,8},{8,16},{16,24},{24,0},{32,40},{40,48},{48,56},{56,32},{64,72... | collective-permute-start | bytes 1572872 | tf_op jit(solution)/shard_map/ppermute | solution.py:289
  12.3 0.8 collective-permute-start.3
  13.1 6.9 %attend_early.1 = (bf16[512,1024]{1,0:T(8,128)(2,1)}, bf16[512,1024]{1,0:T(8,128)(2,1)}, f32[8,512]{1,0:T(8,128)}, f32[256,128]{1,0:T(8,128)}, f32[256,128]{1,0:T(8,128)}, /*index=5*/bf16[256,256]{1,0:T(8,128)(2,1)}) custom-call(bf16[512,1024]{1,0:T(8,128)(2,1)} %q.3, bf16[512,1024]{1,0:T(8,128)(2,1)} %g.3, bf16[512,128]{1,0:T(8,128)(2,1)} %copy-done.18, ...), custom_call_target="tpu_custom_call" | custom-call | flops 1207959552 | bytes 33554432 | tf_op jit(solution)/shard_map/attend_early/pallas_call | solution.py:119
  20.0 3.5 %collective-permute-start.2 = (bf16[256,256]{1,0:T(8,128)(2,1)}, bf16[256,256]{1,0:T(8,128)(2,1)S(1)}, u32[]{:S(2)}, u32[]{:S(2)}) collective-permute-start(bf16[256,256]{1,0:T(8,128)(2,1)} %get-tuple-element.36), channel_id=1, source_target_pairs={{8,0},{16,8},{24,16},{32,24},{40,32},{48,40},{56,48},{64,56},{72,6... | collective-permute-start | bytes 393224 | tf_op jit(solution)/shard_map/ppermute | solution.py:296
  23.5 0.5 collective-permute-start.6
  24.0 3.1 %collective-permute-done.2.back = bf16[256,256]{1,0:T(8,128)(2,1)S(1)} collective-permute-done((bf16[256,256]{1,0:T(8,128)(2,1)}, bf16[256,256]{1,0:T(8,128)(2,1)S(1)}, u32[]{:S(2)}, u32[]{:S(2)}) %collective-permute-start.2) | collective-permute-done | bytes 131104 | tf_op jit(solution)/shard_map/ppermute | solution.py:296
  27.2 1.5 %collective-permute-start.7 = (bf16[512,512]{1,0:T(8,128)(2,1)S(1)}, bf16[512,512]{1,0:T(8,128)(2,1)S(1)}, u32[]{:S(2)}, u32[]{:S(2)}) collective-permute-start(bf16[512,512]{1,0:T(8,128)(2,1)S(1)} %get-tuple-element.46.d0), channel_id=1, source_target_pairs={{0,24},{8,0},{16,8},{24,16},{32,56},{40,32},{48,40},{56,48},{64,88... | collective-permute-start | bytes 1572872 | tf_op jit(solution)/shard_map/ppermute | solution.py:297
  28.7 7.0 %attend_late.1 = (bf16[512,1024]{1,0:T(8,128)(2,1)}, bf16[512,1024]{1,0:T(8,128)(2,1)}, f32[8,512]{1,0:T(8,128)}, bf16[256,256]{1,0:T(8,128)(2,1)}, f32[256,256]{1,0:T(8,128)}) custom-call(bf16[512,1024]{1,0:T(8,128)(2,1)} %q.3, bf16[512,1024]{1,0:T(8,128)(2,1)} %g.3, ...), custom_call_target="tpu_custom_call", output_to_operand_aliasing={{0}: (9, {}), {1}: (10, {}), {2}: (11, {})} | custom-call | flops 1207959552 | bytes 33554432 | tf_op jit(solution)/shard_map/attend_late/pallas_call | solution.py:131
  35.7 0.0 collective-permute-done.4.a1
  35.7 0.0 collective-permute-done.3.a3
  35.7 0.7 collective-permute-start.5
  36.5 1.9 %join_gradients.1 = (bf16[512,256]{1,0:T(8,128)(2,1)}, bf16[512,128]{1,0:T(8,128)(2,1)}, bf16[512,128]{1,0:T(8,128)(2,1)}) custom-call(bf16[256,256]{1,0:T(8,128)(2,1)} %get-tuple-element.34.low, f32[256,256]{1,0:T(8,128)} %get-tuple-element.35.high, bf16[256,256]{1,0:T(8,128)(2,1)} %copy-done.3), custom_call_target="tpu_custom_call" | custom-call | tf_op jit(solution)/shard_map/join_gradients/pallas_call | solution.py:181
  38.4 7.4 %collective-permute-start.12 = (bf16[512,256]{1,0:T(8,128)(2,1)}, bf16[512,256]{1,0:T(8,128)(2,1)S(1)}, u32[]{:S(2)}, u32[]{:S(2)}) collective-permute-start(bf16[512,256]{1,0:T(8,128)(2,1)} %get-tuple-element.47), channel_id=1, source_target_pairs={{0,20},{1,17},{2,22},{3,19},{4,16},{5,21},{6,18},{7,23},{8,26},{9,... | collective-permute-start | bytes 786440 | tf_op jit(solution)/shard_map/ppermute | solution.py:302
  45.8 1.1 collective-permute-start.11
  46.8 0.0 collective-permute-done.6.d1
  46.8 3.5 %collective-permute-start.10 = (bf16[512,256]{1,0:T(8,128)(2,1)}, bf16[512,256]{1,0:T(8,128)(2,1)S(1)}, u32[]{:S(2)}, u32[]{:S(2)}) collective-permute-start(bf16[512,256]{1,0:T(8,128)(2,1)} %get-tuple-element.47), channel_id=1, source_target_pairs={{0,14},{1,11},{2,8},{3,13},{4,10},{5,15},{6,12},{7,9},{8,20},{9,17... | collective-permute-start | bytes 786440 | tf_op jit(solution)/shard_map/ppermute | solution.py:302
  50.3 0.0 collective-permute-done.7.d3
  50.3 3.0 %collective-permute-start.9 = (bf16[512,256]{1,0:T(8,128)(2,1)}, bf16[512,256]{1,0:T(8,128)(2,1)S(1)}, u32[]{:S(2)}, u32[]{:S(2)}) collective-permute-start(bf16[512,256]{1,0:T(8,128)(2,1)} %get-tuple-element.47), channel_id=1, source_target_pairs={{0,0},{1,5},{2,2},{3,7},{4,4},{5,1},{6,6},{7,3},{8,14},{9,11},{10,... | collective-permute-start | bytes 786440 | tf_op jit(solution)/shard_map/ppermute | solution.py:302
  53.3 0.0 collective-permute-done.12.b2
  53.3 6.4 %collective-permute-start.8 = (bf16[512,512]{1,0:T(8,128)(2,1)S(1)}, bf16[512,512]{1,0:T(8,128)(2,1)S(1)}, u32[]{:S(2)}, u32[]{:S(2)}) collective-permute-start(bf16[512,512]{1,0:T(8,128)(2,1)S(1)} %collective-permute-done.7.d3), channel_id=1, source_target_pairs={{0,24},{8,0},{16,8},{24,16},{32,56},{40,32},{48,40},{56,48},{64,88... | collective-permute-start | bytes 1572872 | tf_op jit(solution)/shard_map/ppermute | solution.py:299
  59.7 0.0 collective-permute-done.11.b3
  59.7 0.0 collective-permute-start.16
  59.7 2.2 %collective-permute-done.10.b1 = bf16[512,256]{1,0:T(8,128)(2,1)S(1)} collective-permute-done((bf16[512,256]{1,0:T(8,128)(2,1)}, bf16[512,256]{1,0:T(8,128)(2,1)S(1)}, u32[]{:S(2)}, u32[]{:S(2)}) %collective-permute-start.10) | collective-permute-done | bytes 262176 | tf_op jit(solution)/shard_map/ppermute | solution.py:302
  61.9 0.0 collective-permute-start.15
  61.9 0.0 collective-permute-done.9.b0
  61.9 0.0 copy-start.13
  61.9 0.5 collective-permute-start.14
  62.4 0.0 collective-permute-done.5.a2
  62.4 0.1 collective-permute-start.13
  62.5 0.0 collective-permute-done.16.c2
  62.5 0.9 collective-permute-done.15.c3
  63.4 0.4 collective-permute-done.14.c1
  63.8 0.4 collective-permute-done.13.c0
  64.2 0.3 copy-done.16
  64.5 0.7 copy-done.17
  65.2 4.3 %collective-permute-done.8.d2 = bf16[512,512]{1,0:T(8,128)(2,1)S(1)} collective-permute-done((bf16[512,512]{1,0:T(8,128)(2,1)S(1)}, bf16[512,512]{1,0:T(8,128)(2,1)S(1)}, u32[]{:S(2)}, u32[]{:S(2)}) %collective-permute-start.8) | collective-permute-done | bytes 524320 | tf_op jit(solution)/shard_map/ppermute | solution.py:299
  69.6 0.8 copy-done.9
  70.4 6.7 %weight_partial.1 = bf16[1024,512]{1,0:T(8,128)(2,1)} custom-call(bf16[512,512]{1,0:T(8,128)(2,1)} %copy-done.1, bf16[512,512]{1,0:T(8,128)(2,1)} %copy-done.4, bf16[512,512]{1,0:T(8,128)(2,1)} %copy-done.5, bf16[512,512]{1,0:T(8,128)(2,1)} %copy-done.8, bf16[512,512]{1,0:T(8,128)(2,1)} %copy-done.2, bf16[512,512]{1,0:T(8,128)(2,1)} %copy-done.6, ...), custom_call_target="tpu_custom_call" | custom-call | flops 2147483648 | bytes 8388608 | tf_op jit(solution)/shard_map/weight_partial/pallas_call | solution.py:221
  77.0 38.0 %all_to_all.9.parts = bf16[32,32,512]{2,1,0:T(8,128)(2,1)} all-to-all(bf16[32,32,512]{2,1,0:T(8,128)(2,1)} %bitcast.2), channel_id=1, replica_groups=mesh['dp'=32,'tensor'=8] {'dp'}, dimensions={0} | all-to-all | bytes 2097152 | tf_op jit(solution)/shard_map/all_to_all | solution.py:308
  115.1 2.1 %sum_parts.1 = f32[32,2048]{1,0:T(8,128)} custom-call(bf16[32,32,512]{2,1,0:T(8,128)(2,1)} %all_to_all.9.parts), custom_call_target="tpu_custom_call" | custom-call | flops 524288 | bytes 2097152 | tf_op jit(solution)/shard_map/sum_parts/pallas_call | solution.py:247
  (33 shorter events, 0.1 us)
Async XLA Ops:
  0.6 7.8 %collective-permute-start = (bf16[512,128]{1,0:T(8,128)(2,1)}, bf16[512,128]{1,0:T(8,128)(2,1)S(1)}, u32[]{:S(2)}, u32[]{:S(2)}) collective-permute-start(bf16[512,128]{1,0:T(8,128)(2,1)} %k_hi.3), channel_id=1, source_target_pairs={{0,8},{8,16},{16,24},{24,32},{32,40},{40,48},{48,56},{56,64},{64,7... | collective-permute-start | bytes 393224 | tf_op jit(solution)/shard_map/ppermute | solution.py:284
  4.0 7.1 %collective-permute-start.1 = (bf16[512,128]{1,0:T(8,128)(2,1)}, bf16[512,128]{1,0:T(8,128)(2,1)S(1)}, u32[]{:S(2)}, u32[]{:S(2)}) collective-permute-start(bf16[512,128]{1,0:T(8,128)(2,1)} %v_hi.3), channel_id=1, source_target_pairs={{0,8},{8,16},{16,24},{24,32},{32,40},{40,48},{48,56},{56,64},{64,7... | collective-permute-start | bytes 393224 | tf_op jit(solution)/shard_map/ppermute | solution.py:285
  7.2 1.2 %copy-start = (bf16[512,1024]{1,0:T(8,128)(2,1)S(1)}, bf16[512,1024]{1,0:T(8,128)(2,1)}, u32[]{:S(2)}) copy-start(bf16[512,1024]{1,0:T(8,128)(2,1)} %x.1) | copy-start | bytes 3145732
  8.5 11.6 %copy-start.1 = (bf16[512,512]{1,0:T(8,128)(2,1)}, bf16[512,512]{1,0:T(8,128)(2,1)S(1)}, u32[]{:S(2)}) copy-start(bf16[512,512]{1,0:T(8,128)(2,1)S(1)} %get-tuple-element.38.a0) | copy-start | bytes 1572868
  8.5 18.7 %copy-start.2 = (bf16[512,512]{1,0:T(8,128)(2,1)}, bf16[512,512]{1,0:T(8,128)(2,1)S(1)}, u32[]{:S(2)}) copy-start(bf16[512,512]{1,0:T(8,128)(2,1)S(1)} %get-tuple-element.46.d0) | copy-start | bytes 1572868
  8.5 4.7 %copy-start.18 = (bf16[512,128]{1,0:T(8,128)(2,1)}, bf16[512,128]{1,0:T(8,128)(2,1)S(1)}, u32[]{:S(2)}) copy-start(bf16[512,128]{1,0:T(8,128)(2,1)S(1)} %collective-permute-done.k_lo) | copy-start | bytes 393220
  11.1 2.0 %copy-start.19 = (bf16[512,128]{1,0:T(8,128)(2,1)}, bf16[512,128]{1,0:T(8,128)(2,1)S(1)}, u32[]{:S(2)}) copy-start(bf16[512,128]{1,0:T(8,128)(2,1)S(1)} %collective-permute-done.1.v_lo) | copy-start | bytes 393220
  11.1 24.6 %collective-permute-start.4 = (bf16[512,512]{1,0:T(8,128)(2,1)S(1)}, bf16[512,512]{1,0:T(8,128)(2,1)S(1)}, u32[]{:S(2)}, u32[]{:S(2)}) collective-permute-start(bf16[512,512]{1,0:T(8,128)(2,1)S(1)} %get-tuple-element.38.a0), channel_id=1, source_target_pairs={{0,8},{8,16},{16,24},{24,0},{32,40},{40,48},{48,56},{56,32},{64,72... | collective-permute-start | bytes 1572872 | tf_op jit(solution)/shard_map/ppermute | solution.py:289
  12.3 23.4 %collective-permute-start.3 = (bf16[512,512]{1,0:T(8,128)(2,1)S(1)}, bf16[512,512]{1,0:T(8,128)(2,1)S(1)}, u32[]{:S(2)}, u32[]{:S(2)}) collective-permute-start(bf16[512,512]{1,0:T(8,128)(2,1)S(1)} %get-tuple-element.38.a0), channel_id=1, source_target_pairs={{0,24},{8,0},{16,8},{24,16},{32,56},{40,32},{48,40},{56,48},{64,88... | collective-permute-start | bytes 1572872 | tf_op jit(solution)/shard_map/ppermute | solution.py:290
  20.0 7.1 %collective-permute-start.2 = (bf16[256,256]{1,0:T(8,128)(2,1)}, bf16[256,256]{1,0:T(8,128)(2,1)S(1)}, u32[]{:S(2)}, u32[]{:S(2)}) collective-permute-start(bf16[256,256]{1,0:T(8,128)(2,1)} %get-tuple-element.36), channel_id=1, source_target_pairs={{8,0},{16,8},{24,16},{32,24},{40,32},{48,40},{56,48},{64,56},{72,6... | collective-permute-start | bytes 393224 | tf_op jit(solution)/shard_map/ppermute | solution.py:296
  23.5 23.3 %collective-permute-start.6 = (bf16[512,512]{1,0:T(8,128)(2,1)S(1)}, bf16[512,512]{1,0:T(8,128)(2,1)S(1)}, u32[]{:S(2)}, u32[]{:S(2)}) collective-permute-start(bf16[512,512]{1,0:T(8,128)(2,1)S(1)} %get-tuple-element.46.d0), channel_id=1, source_target_pairs={{0,8},{8,16},{16,24},{24,0},{32,40},{40,48},{48,56},{56,32},{64,72... | collective-permute-start | bytes 1572872 | tf_op jit(solution)/shard_map/ppermute | solution.py:295
  27.2 8.5 %copy-start.3 = (bf16[256,256]{1,0:T(8,128)(2,1)}, bf16[256,256]{1,0:T(8,128)(2,1)S(1)}, u32[]{:S(2)}) copy-start(bf16[256,256]{1,0:T(8,128)(2,1)S(1)} %collective-permute-done.2.back) | copy-start | bytes 393220
  27.2 23.1 %collective-permute-start.7 = (bf16[512,512]{1,0:T(8,128)(2,1)S(1)}, bf16[512,512]{1,0:T(8,128)(2,1)S(1)}, u32[]{:S(2)}, u32[]{:S(2)}) collective-permute-start(bf16[512,512]{1,0:T(8,128)(2,1)S(1)} %get-tuple-element.46.d0), channel_id=1, source_target_pairs={{0,24},{8,0},{16,8},{24,16},{32,56},{40,32},{48,40},{56,48},{64,88... | collective-permute-start | bytes 1572872 | tf_op jit(solution)/shard_map/ppermute | solution.py:297
  35.7 33.8 %copy-start.4 = (bf16[512,512]{1,0:T(8,128)(2,1)}, bf16[512,512]{1,0:T(8,128)(2,1)S(1)}, u32[]{:S(2)}) copy-start(bf16[512,512]{1,0:T(8,128)(2,1)S(1)} %collective-permute-done.4.a1) | copy-start | bytes 1572868
  35.7 33.8 %copy-start.5 = (bf16[512,512]{1,0:T(8,128)(2,1)}, bf16[512,512]{1,0:T(8,128)(2,1)S(1)}, u32[]{:S(2)}) copy-start(bf16[512,512]{1,0:T(8,128)(2,1)S(1)} %collective-permute-done.3.a3) | copy-start | bytes 1572868
  35.7 26.7 %collective-permute-start.5 = (bf16[512,512]{1,0:T(8,128)(2,1)S(1)}, bf16[512,512]{1,0:T(8,128)(2,1)S(1)}, u32[]{:S(2)}, u32[]{:S(2)}) collective-permute-start(bf16[512,512]{1,0:T(8,128)(2,1)S(1)} %collective-permute-done.4.a1), channel_id=1, source_target_pairs={{0,8},{8,16},{16,24},{24,0},{32,40},{40,48},{48,56},{56,32},{64,72... | collective-permute-start | bytes 1572872 | tf_op jit(solution)/shard_map/ppermute | solution.py:298
  38.4 14.9 %collective-permute-start.12 = (bf16[512,256]{1,0:T(8,128)(2,1)}, bf16[512,256]{1,0:T(8,128)(2,1)S(1)}, u32[]{:S(2)}, u32[]{:S(2)}) collective-permute-start(bf16[512,256]{1,0:T(8,128)(2,1)} %get-tuple-element.47), channel_id=1, source_target_pairs={{0,20},{1,17},{2,22},{3,19},{4,16},{5,21},{6,18},{7,23},{8,26},{9,... | collective-permute-start | bytes 786440 | tf_op jit(solution)/shard_map/ppermute | solution.py:302
  45.8 13.9 %collective-permute-start.11 = (bf16[512,256]{1,0:T(8,128)(2,1)}, bf16[512,256]{1,0:T(8,128)(2,1)S(1)}, u32[]{:S(2)}, u32[]{:S(2)}) collective-permute-start(bf16[512,256]{1,0:T(8,128)(2,1)} %get-tuple-element.47), channel_id=1, source_target_pairs={{0,26},{1,31},{2,28},{3,25},{4,30},{5,27},{6,24},{7,29},{8,0},{9,5... | collective-permute-start | bytes 786440 | tf_op jit(solution)/shard_map/ppermute | solution.py:302
  46.8 22.7 %copy-start.6 = (bf16[512,512]{1,0:T(8,128)(2,1)}, bf16[512,512]{1,0:T(8,128)(2,1)S(1)}, u32[]{:S(2)}) copy-start(bf16[512,512]{1,0:T(8,128)(2,1)S(1)} %collective-permute-done.6.d1) | copy-start | bytes 1572868
  46.8 15.1 %collective-permute-start.10 = (bf16[512,256]{1,0:T(8,128)(2,1)}, bf16[512,256]{1,0:T(8,128)(2,1)S(1)}, u32[]{:S(2)}, u32[]{:S(2)}) collective-permute-start(bf16[512,256]{1,0:T(8,128)(2,1)} %get-tuple-element.47), channel_id=1, source_target_pairs={{0,14},{1,11},{2,8},{3,13},{4,10},{5,15},{6,12},{7,9},{8,20},{9,17... | collective-permute-start | bytes 786440 | tf_op jit(solution)/shard_map/ppermute | solution.py:302
  50.3 19.2 %copy-start.7 = (bf16[512,512]{1,0:T(8,128)(2,1)}, bf16[512,512]{1,0:T(8,128)(2,1)S(1)}, u32[]{:S(2)}) copy-start(bf16[512,512]{1,0:T(8,128)(2,1)S(1)} %collective-permute-done.7.d3) | copy-start | bytes 1572868
  50.3 11.6 %collective-permute-start.9 = (bf16[512,256]{1,0:T(8,128)(2,1)}, bf16[512,256]{1,0:T(8,128)(2,1)S(1)}, u32[]{:S(2)}, u32[]{:S(2)}) collective-permute-start(bf16[512,256]{1,0:T(8,128)(2,1)} %get-tuple-element.47), channel_id=1, source_target_pairs={{0,0},{1,5},{2,2},{3,7},{4,4},{5,1},{6,6},{7,3},{8,14},{9,11},{10,... | collective-permute-start | bytes 786440 | tf_op jit(solution)/shard_map/ppermute | solution.py:302
  53.3 16.2 %copy-start.10 = (bf16[512,256]{1,0:T(8,128)(2,1)}, bf16[512,256]{1,0:T(8,128)(2,1)S(1)}, u32[]{:S(2)}) copy-start(bf16[512,256]{1,0:T(8,128)(2,1)S(1)} %collective-permute-done.12.b2) | copy-start | bytes 786436
  53.3 16.2 %collective-permute-start.8 = (bf16[512,512]{1,0:T(8,128)(2,1)S(1)}, bf16[512,512]{1,0:T(8,128)(2,1)S(1)}, u32[]{:S(2)}, u32[]{:S(2)}) collective-permute-start(bf16[512,512]{1,0:T(8,128)(2,1)S(1)} %collective-permute-done.7.d3), channel_id=1, source_target_pairs={{0,24},{8,0},{16,8},{24,16},{32,56},{40,32},{48,40},{56,48},{64,88... | collective-permute-start | bytes 1572872 | tf_op jit(solution)/shard_map/ppermute | solution.py:299
  59.7 4.1 %copy-start.11 = (bf16[512,256]{1,0:T(8,128)(2,1)}, bf16[512,256]{1,0:T(8,128)(2,1)S(1)}, u32[]{:S(2)}) copy-start(bf16[512,256]{1,0:T(8,128)(2,1)S(1)} %collective-permute-done.11.b3) | copy-start | bytes 786436
  59.7 2.9 %collective-permute-start.16 = (bf16[512,256]{1,0:T(8,128)(2,1)S(1)}, bf16[512,256]{1,0:T(8,128)(2,1)S(1)}, u32[]{:S(2)}, u32[]{:S(2)}) collective-permute-start(bf16[512,256]{1,0:T(8,128)(2,1)S(1)} %collective-permute-done.12.b2), channel_id=1, source_target_pairs={{0,1},{1,0},{2,3},{3,2},{4,5},{5,4},{6,7},{7,6},{8,9},{9,8},{10,11... | collective-permute-start | bytes 786440 | tf_op jit(solution)/shard_map/ppermute | solution.py:304
  61.9 2.3 %copy-start.12 = (bf16[512,256]{1,0:T(8,128)(2,1)}, bf16[512,256]{1,0:T(8,128)(2,1)S(1)}, u32[]{:S(2)}) copy-start(bf16[512,256]{1,0:T(8,128)(2,1)S(1)} %collective-permute-done.10.b1) | copy-start | bytes 786436
  61.9 1.5 %collective-permute-start.15 = (bf16[512,256]{1,0:T(8,128)(2,1)S(1)}, bf16[512,256]{1,0:T(8,128)(2,1)S(1)}, u32[]{:S(2)}, u32[]{:S(2)}) collective-permute-start(bf16[512,256]{1,0:T(8,128)(2,1)S(1)} %collective-permute-done.11.b3), channel_id=1, source_target_pairs={{0,1},{1,0},{2,3},{3,2},{4,5},{5,4},{6,7},{7,6},{8,9},{9,8},{10,11... | collective-permute-start | bytes 786440 | tf_op jit(solution)/shard_map/ppermute | solution.py:304
  61.9 7.6 %copy-start.13 = (bf16[512,256]{1,0:T(8,128)(2,1)}, bf16[512,256]{1,0:T(8,128)(2,1)S(1)}, u32[]{:S(2)}) copy-start(bf16[512,256]{1,0:T(8,128)(2,1)S(1)} %collective-permute-done.9.b0) | copy-start | bytes 786436
  61.9 1.9 %collective-permute-start.14 = (bf16[512,256]{1,0:T(8,128)(2,1)S(1)}, bf16[512,256]{1,0:T(8,128)(2,1)S(1)}, u32[]{:S(2)}, u32[]{:S(2)}) collective-permute-start(bf16[512,256]{1,0:T(8,128)(2,1)S(1)} %collective-permute-done.10.b1), channel_id=1, source_target_pairs={{0,1},{1,0},{2,3},{3,2},{4,5},{5,4},{6,7},{7,6},{8,9},{9,8},{10,11... | collective-permute-start | bytes 786440 | tf_op jit(solution)/shard_map/ppermute | solution.py:304
  62.4 7.1 %copy-start.8 = (bf16[512,512]{1,0:T(8,128)(2,1)}, bf16[512,512]{1,0:T(8,128)(2,1)S(1)}, u32[]{:S(2)}) copy-start(bf16[512,512]{1,0:T(8,128)(2,1)S(1)} %collective-permute-done.5.a2) | copy-start | bytes 1572868
  62.4 1.8 %collective-permute-start.13 = (bf16[512,256]{1,0:T(8,128)(2,1)S(1)}, bf16[512,256]{1,0:T(8,128)(2,1)S(1)}, u32[]{:S(2)}, u32[]{:S(2)}) collective-permute-start(bf16[512,256]{1,0:T(8,128)(2,1)S(1)} %collective-permute-done.9.b0), channel_id=1, source_target_pairs={{0,1},{1,0},{2,3},{3,2},{4,5},{5,4},{6,7},{7,6},{8,9},{9,8},{10,11... | collective-permute-start | bytes 786440 | tf_op jit(solution)/shard_map/ppermute | solution.py:304
  62.5 7.0 %copy-start.14 = (bf16[512,256]{1,0:T(8,128)(2,1)}, bf16[512,256]{1,0:T(8,128)(2,1)S(1)}, u32[]{:S(2)}) copy-start(bf16[512,256]{1,0:T(8,128)(2,1)S(1)} %collective-permute-done.16.c2) | copy-start | bytes 786436
  63.4 0.8 copy-start.15
  63.8 0.7 copy-start.16
  64.5 0.7 copy-start.17
  69.6 0.8 copy-start.9

commit v3 on v2

--- a/solution.py
+++ b/solution.py
@@ -101,7 +101,7 @@
     return pl.BlockSpec(shape, lambda i: at)
 
 
-def attention(queries, out_grad, key_rows, value_matrix, prior_keys, prior_vals, docs):
+def attention(queries, out_grad, key_rows, value_matrix, prior, docs):
     tok, width = queries.shape
     heads = width // HEAD
     half = tok // 2
@@ -119,14 +119,14 @@
     o, dq, lse, dk_own, dv_own, back = pl.pallas_call(
         early_kernel,
         grid=(1,),
-        in_specs=[wide(0), wide(0), kv(1), kv(0), kv(1), kv(0), doc],
+        in_specs=[wide(0), wide(0), kv(0), kv(0), spec((half, HEAD), (0, 1)), kv(0), doc],
         out_specs=[wide(0), wide(0), spec((heads, half), (0, 0)), part, part, pair],
         out_shape=[rows_out, rows_out, lse_out, grad, grad, jax.ShapeDtypeStruct((half, 2 * HEAD), BF16)],
         scratch_shapes=scratch,
         cost_estimate=cost,
         compiler_params=params,
         name="attend_early",
-    )(queries, out_grad, prior_keys, key_rows, prior_vals, value_matrix, docs)
+    )(queries, out_grad, prior, key_rows, prior, value_matrix, docs)
     hbm = pl.BlockSpec(memory_space=pl.ANY)
     o, dq, lse, low, high = pl.pallas_call(
         late_kernel,
@@ -143,20 +143,38 @@
     return o, dq, lse, back, low, high, dk_own
 
 
+def tail_kernel(k, v, out):
+    out[:, :HEAD] = k[...]
+    out[:, HEAD:] = v[...]
+
+
+def pack_tail(key_rows, value_matrix):
+    half = key_rows.shape[0] // 2
+    return pl.pallas_call(
+        tail_kernel,
+        grid=(1,),
+        in_specs=[spec((half, HEAD), (1, 0))] * 2,
+        out_specs=spec((half, 2 * HEAD), (0, 0)),
+        out_shape=jax.ShapeDtypeStruct((half, 2 * HEAD), BF16),
+        name="pack_tail",
+    )(key_rows, value_matrix)
+
+
 def split_kernel(x, first, second):
-    half = first.shape[1]
-    first[...] = x[:, :half]
-    second[...] = x[:, half:]
+    half = first.shape[0]
+    first[...] = x[:, :half].T
+    second[...] = x[:, half:].T
 
 
 def split_inputs(inputs):
     tok, width = inputs.shape
-    part = jax.ShapeDtypeStruct((tok, width // 2), BF16)
+    shape = (width // 2, tok)
+    part = jax.ShapeDtypeStruct(shape, BF16)
     return pl.pallas_call(
         split_kernel,
         grid=(1,),
         in_specs=[spec((tok, width), (0, 0))],
-        out_specs=[spec((tok, width // 2), (0, 0))] * 2,
+        out_specs=[spec(shape, (0, 0))] * 2,
         out_shape=[part, part],
         compiler_params=pltpu.CompilerParams(vmem_limit_bytes=48 << 20),
         name="split_inputs",
@@ -194,11 +212,10 @@
     other = pl.ds(pl.multiple_of((1 - core) * 2 * HEAD, 2 * HEAD), 2 * HEAD)
 
     def multiply(left):
-        for cols, right in ((mine, (b0, b1, b3, b2)), (other, (c0, c1, c3, c2))):
-            total = dot(left[0][...], right[0][...], TN)
-            for l, r in zip(left[1:], right[1:]):
-                total += dot(l[...], r[...], TN)
-            out[:, cols] = total.astype(BF16)
+        right = [jnp.concatenate([b[...], c[...]], axis=1) for b, c in zip((b0, b1, b3, b2), (c0, c1, c3, c2))]
+        total = dot(jnp.concatenate([l[...] for l in left], axis=1), jnp.concatenate(right, axis=0))
+        out[:, mine] = total[:, : 2 * HEAD].astype(BF16)
+        out[:, other] = total[:, 2 * HEAD :].astype(BF16)
 
     steps = pl.num_programs(0) // 2
 
@@ -212,11 +229,11 @@
 
 
 def weight_partial(first, second, mine, other):
-    tile = 2 * HEAD
-    tok, width = first[0].shape
+    tile = 4 * HEAD
+    width, tok = first[0].shape
     steps = width // tile
-    low = pl.BlockSpec((tok, tile), lambda i: (0, jnp.minimum(i, steps - 1)))
-    high = pl.BlockSpec((tok, tile), lambda i: (0, jnp.maximum(i - steps, 0)))
+    low = pl.BlockSpec((tile, tok), lambda i: (jnp.minimum(i, steps - 1), 0))
+    high = pl.BlockSpec((tile, tok), lambda i: (jnp.maximum(i - steps, 0), 0))
     whole = pl.BlockSpec((tok, 2 * HEAD), lambda i: (0, 0))
     return pl.pallas_call(
         weight_kernel,
@@ -281,16 +298,15 @@
     docs = doc_ids.reshape(-1, BLOCK)
     onward = [(i, i + 1) for i in range(shards - 1)]
     backward = [(i + 1, i) for i in range(shards - 1)]
-    prior_keys = lax.ppermute(key_rows, "dp", onward)
-    prior_vals = lax.ppermute(value_matrix, "dp", onward)
+    prior = lax.ppermute(pack_tail(key_rows, value_matrix), "dp", onward)
 
     first, second = split_inputs(inputs)
-    first_sent = after(first, prior_keys, prior_vals)
+    first_sent = after(first, prior)
     first_left = lax.ppermute(first_sent, "dp", along_x(1))
     first_right = lax.ppermute(first_sent, "dp", along_x(-1))
 
     out_rows, query_grad, logsum, back, low, high, dk_early = attention(
-        queries, out_grad, key_rows, value_matrix, prior_keys, prior_vals, docs
+        queries, out_grad, key_rows, value_matrix, prior, docs
     )
     second_left = lax.ppermute(after(second, dk_early), "dp", along_x(1))
     back = lax.ppermute(back, "dp", backward)

time: 118 us -> 116 us (0.983)
  starting transfers between devices: 36.7 us -> 33.2 us
  Pallas kernels: 24.5 us -> 25.8 us
    ppermute x2 -> x1, starting transfers between devices: 6.51 us -> 3.39 us  [body(): prior = lax.ppermute(pack_tail(key_rows, value_matrix), 'dp', onward)]
    pallas_call x1 -> x2, Pallas kernels: 6.87 us -> 8.41 us  [the longest x1 6.86 us: attention(): pl.pallas_call(early_kernel, grid=(1,), in_specs=[wide(0), wide(0), kv(0)...]
    ppermute x2 -> x1, waiting for transfers between devices: 2.62 us -> 2.36 us  [body(): prior = lax.ppermute(pack_tail(key_rows, value_matrix), 'dp', onward)]
    unnamed x40 -> x38, local copies, waits for them, and re-layouts: 3.14 us -> 3.12 us
  transfers between devices with their start and end apart: 17 -> 16, of which waited for: 7 -> 7; matrix products, arithmetic and copies ran while one was open for 0% -> 0% of each run, Pallas kernels for 13% -> 14%
where the time goes in v3:
time: 116 us; the launch traced here: 115 us
  blocking collectives  38 us (33%)
  starting transfers between devices  33.2 us (29%)
  Pallas kernels  25.8 us (22%)
  waiting for transfers between devices  14.4 us (12%)
  local copies, waits for them, and re-layouts  3.12 us (3%)
    all_to_all x1, blocking collectives, body(): parts = lax.all_to_all(partial, 'dp', 0, 0, tiled=True)  38 us
    ppermute x4, starting transfers between devices, body(): lax.ppermute(joined, ('dp', 'tensor'), to_columns(d))  14.1 us
    pallas_call x1, Pallas kernels, attention(): pl.pallas_call(late_kernel, grid=(1,), in_specs=[wide(1), wide(1), kv(0),...  6.99 us
    ppermute x1, starting transfers between devices, body(): second_far = lax.ppermute(second_right, 'dp', along_x(-1))  6.92 us
    pallas_call x1, Pallas kernels, attention(): pl.pallas_call(early_kernel, grid=(1,), in_specs=[wide(0), wide(0), kv(0)...  6.86 us
    pallas_call x1, Pallas kernels, weight_partial(): pl.pallas_call(weight_kernel, grid=(2 * steps,), in_specs=[low] * 4 + [hi...  6.2 us
    ppermute x1, waiting for transfers between devices, body(): second_far = lax.ppermute(second_right, 'dp', along_x(-1))  4.32 us
    ppermute x1, waiting for transfers between devices, body(): back = lax.ppermute(back, 'dp', backward)  3.91 us
  transfers between devices with their start and end apart: 16, of which 7 were waited for; matrix products, arithmetic and copies ran while one was open for 0% of the time, Pallas kernels for 14%

profile of v3, /device:TPU:2, one launch (start us, length us, event | category | flops | bytes accessed | tf_op | source)
XLA Modules:
  0.0 115.4 jit_solution(9923178797031651248)
XLA Ops:
  0.6 1.6 %pack_tail.1 = bf16[256,256]{1,0:T(8,128)(2,1)} custom-call(bf16[512,128]{1,0:T(8,128)(2,1)} %k_hi.3, bf16[512,128]{1,0:T(8,128)(2,1)} %v_hi.3), custom_call_target="tpu_custom_call" | custom-call | tf_op jit(solution)/shard_map/pack_tail/pallas_call | solution.py:153
  2.2 3.4 %collective-permute-start = (bf16[256,256]{1,0:T(8,128)(2,1)}, bf16[256,256]{1,0:T(8,128)(2,1)S(1)}, u32[]{:S(2)}, u32[]{:S(2)}) collective-permute-start(bf16[256,256]{1,0:T(8,128)(2,1)} %pack_tail.1), channel_id=1, source_target_pairs={{0,8},{8,16},{16,24},{24,32},{32,40},{40,48},{48,56},{56,64},{64,7... | collective-permute-start | bytes 393224 | tf_op jit(solution)/shard_map/ppermute | solution.py:301
  5.6 0.0 copy-start
  5.6 1.2 %copy-done = bf16[512,1024]{1,0:T(8,128)(2,1)S(1)} copy-done((bf16[512,1024]{1,0:T(8,128)(2,1)S(1)}, bf16[512,1024]{1,0:T(8,128)(2,1)}, u32[]{:S(2)}) %copy-start) | copy-done | bytes 1048600
  6.8 0.3 split_inputs.1
  7.2 2.4 %collective-permute-done.k_lo.v_lo = bf16[256,256]{1,0:T(8,128)(2,1)S(1)} collective-permute-done((bf16[256,256]{1,0:T(8,128)(2,1)}, bf16[256,256]{1,0:T(8,128)(2,1)S(1)}, u32[]{:S(2)}, u32[]{:S(2)}) %collective-permute-start) | collective-permute-done | bytes 131104 | tf_op jit(solution)/shard_map/ppermute | solution.py:301
  9.5 1.5 %collective-permute-start.3 = (bf16[512,512]{1,0:T(8,128)(2,1)S(1)}, bf16[512,512]{1,0:T(8,128)(2,1)S(1)}, u32[]{:S(2)}, u32[]{:S(2)}) collective-permute-start(bf16[512,512]{1,0:T(8,128)(2,1)S(1)} %get-tuple-element.38.a0), channel_id=1, source_target_pairs={{0,8},{8,16},{16,24},{24,0},{32,40},{40,48},{48,56},{56,32},{64,72... | collective-permute-start | bytes 1572872 | tf_op jit(solution)/shard_map/ppermute | solution.py:305
  11.0 0.5 collective-permute-start.2
  11.5 6.9 %attend_early.1 = (bf16[512,1024]{1,0:T(8,128)(2,1)}, bf16[512,1024]{1,0:T(8,128)(2,1)}, f32[8,512]{1,0:T(8,128)}, f32[256,128]{1,0:T(8,128)}, f32[256,128]{1,0:T(8,128)}, /*index=5*/bf16[256,256]{1,0:T(8,128)(2,1)}) custom-call(bf16[512,1024]{1,0:T(8,128)(2,1)} %q.3, bf16[512,1024]{1,0:T(8,128)(2,1)} %g.3, bf16[256,256]{1,0:T(8,128)(2,1)} %copy-done.18, ...), custom_call_target="tpu_custom_call" | custom-call | flops 1207959552 | bytes 33554432 | tf_op jit(solution)/shard_map/attend_early/pallas_call | solution.py:119
  18.4 0.0 copy-done.1
  18.4 3.2 %collective-permute-start.1 = (bf16[256,256]{1,0:T(8,128)(2,1)}, bf16[256,256]{1,0:T(8,128)(2,1)S(1)}, u32[]{:S(2)}, u32[]{:S(2)}) collective-permute-start(bf16[256,256]{1,0:T(8,128)(2,1)} %get-tuple-element.36), channel_id=1, source_target_pairs={{8,0},{16,8},{24,16},{32,24},{40,32},{48,40},{56,48},{64,56},{72,6... | collective-permute-start | bytes 393224 | tf_op jit(solution)/shard_map/ppermute | solution.py:312
  21.6 0.8 collective-permute-start.5
  22.4 3.9 %collective-permute-done.1.back = bf16[256,256]{1,0:T(8,128)(2,1)S(1)} collective-permute-done((bf16[256,256]{1,0:T(8,128)(2,1)}, bf16[256,256]{1,0:T(8,128)(2,1)S(1)}, u32[]{:S(2)}, u32[]{:S(2)}) %collective-permute-start.1) | collective-permute-done | bytes 131104 | tf_op jit(solution)/shard_map/ppermute | solution.py:312
  26.3 0.5 collective-permute-start.6
  26.9 7.0 %attend_late.1 = (bf16[512,1024]{1,0:T(8,128)(2,1)}, bf16[512,1024]{1,0:T(8,128)(2,1)}, f32[8,512]{1,0:T(8,128)}, bf16[256,256]{1,0:T(8,128)(2,1)}, f32[256,256]{1,0:T(8,128)}) custom-call(bf16[512,1024]{1,0:T(8,128)(2,1)} %q.3, bf16[512,1024]{1,0:T(8,128)(2,1)} %g.3, ...), custom_call_target="tpu_custom_call", output_to_operand_aliasing={{0}: (9, {}), {1}: (10, {}), {2}: (11, {})} | custom-call | flops 1207959552 | bytes 33554432 | tf_op jit(solution)/shard_map/attend_late/pallas_call | solution.py:131
  33.9 0.0 collective-permute-done.3.a1
  33.9 0.0 collective-permute-done.2.a3
  33.9 1.6 %collective-permute-start.4 = (bf16[512,512]{1,0:T(8,128)(2,1)S(1)}, bf16[512,512]{1,0:T(8,128)(2,1)S(1)}, u32[]{:S(2)}, u32[]{:S(2)}) collective-permute-start(bf16[512,512]{1,0:T(8,128)(2,1)S(1)} %collective-permute-done.3.a1), channel_id=1, source_target_pairs={{0,8},{8,16},{16,24},{24,0},{32,40},{40,48},{48,56},{56,32},{64,72... | collective-permute-start | bytes 1572872 | tf_op jit(solution)/shard_map/ppermute | solution.py:314
  35.5 1.9 %join_gradients.1 = (bf16[512,256]{1,0:T(8,128)(2,1)}, bf16[512,128]{1,0:T(8,128)(2,1)}, bf16[512,128]{1,0:T(8,128)(2,1)}) custom-call(bf16[256,256]{1,0:T(8,128)(2,1)} %get-tuple-element.34.low, f32[256,256]{1,0:T(8,128)} %get-tuple-element.35.high, bf16[256,256]{1,0:T(8,128)(2,1)} %copy-done.3), custom_call_target="tpu_custom_call" | custom-call | tf_op jit(solution)/shard_map/join_gradients/pallas_call | solution.py:199
  37.3 6.6 %collective-permute-start.11 = (bf16[512,256]{1,0:T(8,128)(2,1)}, bf16[512,256]{1,0:T(8,128)(2,1)S(1)}, u32[]{:S(2)}, u32[]{:S(2)}) collective-permute-start(bf16[512,256]{1,0:T(8,128)(2,1)} %get-tuple-element.47), channel_id=1, source_target_pairs={{0,20},{1,17},{2,22},{3,19},{4,16},{5,21},{6,18},{7,23},{8,26},{9,... | collective-permute-start | bytes 786440 | tf_op jit(solution)/shard_map/ppermute | solution.py:318
  44.0 1.1 collective-permute-start.10
  45.0 0.0 collective-permute-done.5.d1
  45.0 3.5 %collective-permute-start.9 = (bf16[512,256]{1,0:T(8,128)(2,1)}, bf16[512,256]{1,0:T(8,128)(2,1)S(1)}, u32[]{:S(2)}, u32[]{:S(2)}) collective-permute-start(bf16[512,256]{1,0:T(8,128)(2,1)} %get-tuple-element.47), channel_id=1, source_target_pairs={{0,14},{1,11},{2,8},{3,13},{4,10},{5,15},{6,12},{7,9},{8,20},{9,17... | collective-permute-start | bytes 786440 | tf_op jit(solution)/shard_map/ppermute | solution.py:318
  48.5 0.0 collective-permute-done.6.d3
  48.5 3.0 %collective-permute-start.8 = (bf16[512,256]{1,0:T(8,128)(2,1)}, bf16[512,256]{1,0:T(8,128)(2,1)S(1)}, u32[]{:S(2)}, u32[]{:S(2)}) collective-permute-start(bf16[512,256]{1,0:T(8,128)(2,1)} %get-tuple-element.47), channel_id=1, source_target_pairs={{0,0},{1,5},{2,2},{3,7},{4,4},{5,1},{6,6},{7,3},{8,14},{9,11},{10,... | collective-permute-start | bytes 786440 | tf_op jit(solution)/shard_map/ppermute | solution.py:318
  51.5 0.0 collective-permute-done.11.b2
  51.5 6.9 %collective-permute-start.7 = (bf16[512,512]{1,0:T(8,128)(2,1)S(1)}, bf16[512,512]{1,0:T(8,128)(2,1)S(1)}, u32[]{:S(2)}, u32[]{:S(2)}) collective-permute-start(bf16[512,512]{1,0:T(8,128)(2,1)S(1)} %collective-permute-done.6.d3), channel_id=1, source_target_pairs={{0,24},{8,0},{16,8},{24,16},{32,56},{40,32},{48,40},{56,48},{64,88... | collective-permute-start | bytes 1572872 | tf_op jit(solution)/shard_map/ppermute | solution.py:315
  58.4 0.0 collective-permute-done.10.b3
  58.4 0.0 collective-permute-start.15
  58.4 2.2 %collective-permute-done.9.b1 = bf16[512,256]{1,0:T(8,128)(2,1)S(1)} collective-permute-done((bf16[512,256]{1,0:T(8,128)(2,1)}, bf16[512,256]{1,0:T(8,128)(2,1)S(1)}, u32[]{:S(2)}, u32[]{:S(2)}) %collective-permute-start.9) | collective-permute-done | bytes 262176 | tf_op jit(solution)/shard_map/ppermute | solution.py:318
  60.6 0.0 collective-permute-start.14
  60.6 0.0 collective-permute-done.8.b0
  60.6 0.0 copy-start.13
  60.6 0.5 collective-permute-start.13
  61.1 0.0 collective-permute-done.4.a2
  61.1 0.1 collective-permute-start.12
  61.2 0.0 collective-permute-done.15.c2
  61.2 0.9 collective-permute-done.14.c3
  62.1 0.4 collective-permute-done.13.c1
  62.5 0.4 collective-permute-done.12.c0
  62.9 0.0 copy-done.14
  62.9 0.3 copy-done.16
  63.2 0.7 copy-done.17
  63.9 4.3 %collective-permute-done.7.d2 = bf16[512,512]{1,0:T(8,128)(2,1)S(1)} collective-permute-done((bf16[512,512]{1,0:T(8,128)(2,1)S(1)}, bf16[512,512]{1,0:T(8,128)(2,1)S(1)}, u32[]{:S(2)}, u32[]{:S(2)}) %collective-permute-start.7) | collective-permute-done | bytes 524320 | tf_op jit(solution)/shard_map/ppermute | solution.py:315
  68.3 0.8 copy-done.9
  69.1 6.2 %weight_partial.1 = bf16[1024,512]{1,0:T(8,128)(2,1)} custom-call(bf16[512,512]{1,0:T(8,128)(2,1)} %copy-done.1, bf16[512,512]{1,0:T(8,128)(2,1)} %copy-done.4, bf16[512,512]{1,0:T(8,128)(2,1)} %copy-done.5, bf16[512,512]{1,0:T(8,128)(2,1)} %copy-done.8, bf16[512,512]{1,0:T(8,128)(2,1)} %copy-done.2, bf16[512,512]{1,0:T(8,128)(2,1)} %copy-done.6, ...), custom_call_target="tpu_custom_call" | custom-call | flops 2147483648 | bytes 8388608 | tf_op jit(solution)/shard_map/weight_partial/pallas_call | solution.py:238
  75.3 38.0 %all_to_all.9.parts = bf16[32,32,512]{2,1,0:T(8,128)(2,1)} all-to-all(bf16[32,32,512]{2,1,0:T(8,128)(2,1)} %bitcast.2), channel_id=1, replica_groups=mesh['dp'=32,'tensor'=8] {'dp'}, dimensions={0} | all-to-all | bytes 2097152 | tf_op jit(solution)/shard_map/all_to_all | solution.py:324
  113.3 2.1 %sum_parts.1 = f32[32,2048]{1,0:T(8,128)} custom-call(bf16[32,32,512]{2,1,0:T(8,128)(2,1)} %all_to_all.9.parts), custom_call_target="tpu_custom_call" | custom-call | flops 524288 | bytes 2097152 | tf_op jit(solution)/shard_map/sum_parts/pallas_call | solution.py:264
  (30 shorter events, 0.1 us)
Async XLA Ops:
  2.2 7.3 %collective-permute-start = (bf16[256,256]{1,0:T(8,128)(2,1)}, bf16[256,256]{1,0:T(8,128)(2,1)S(1)}, u32[]{:S(2)}, u32[]{:S(2)}) collective-permute-start(bf16[256,256]{1,0:T(8,128)(2,1)} %pack_tail.1), channel_id=1, source_target_pairs={{0,8},{8,16},{16,24},{24,32},{32,40},{40,48},{48,56},{56,64},{64,7... | collective-permute-start | bytes 393224 | tf_op jit(solution)/shard_map/ppermute | solution.py:301
  5.6 1.2 %copy-start = (bf16[512,1024]{1,0:T(8,128)(2,1)S(1)}, bf16[512,1024]{1,0:T(8,128)(2,1)}, u32[]{:S(2)}) copy-start(bf16[512,1024]{1,0:T(8,128)(2,1)} %x.1) | copy-start | bytes 3145732
  7.1 11.3 %copy-start.1 = (bf16[512,512]{1,0:T(8,128)(2,1)}, bf16[512,512]{1,0:T(8,128)(2,1)S(1)}, u32[]{:S(2)}) copy-start(bf16[512,512]{1,0:T(8,128)(2,1)S(1)} %get-tuple-element.38.a0) | copy-start | bytes 1572868
  7.1 19.2 %copy-start.2 = (bf16[512,512]{1,0:T(8,128)(2,1)}, bf16[512,512]{1,0:T(8,128)(2,1)S(1)}, u32[]{:S(2)}) copy-start(bf16[512,512]{1,0:T(8,128)(2,1)S(1)} %get-tuple-element.46.d0) | copy-start | bytes 1572868
  9.5 2.0 %copy-start.18 = (bf16[256,256]{1,0:T(8,128)(2,1)}, bf16[256,256]{1,0:T(8,128)(2,1)S(1)}, u32[]{:S(2)}) copy-start(bf16[256,256]{1,0:T(8,128)(2,1)S(1)} %collective-permute-done.k_lo.v_lo) | copy-start | bytes 393220
  9.5 24.4 %collective-permute-start.3 = (bf16[512,512]{1,0:T(8,128)(2,1)S(1)}, bf16[512,512]{1,0:T(8,128)(2,1)S(1)}, u32[]{:S(2)}, u32[]{:S(2)}) collective-permute-start(bf16[512,512]{1,0:T(8,128)(2,1)S(1)} %get-tuple-element.38.a0), channel_id=1, source_target_pairs={{0,8},{8,16},{16,24},{24,0},{32,40},{40,48},{48,56},{56,32},{64,72... | collective-permute-start | bytes 1572872 | tf_op jit(solution)/shard_map/ppermute | solution.py:305
  11.0 22.9 %collective-permute-start.2 = (bf16[512,512]{1,0:T(8,128)(2,1)S(1)}, bf16[512,512]{1,0:T(8,128)(2,1)S(1)}, u32[]{:S(2)}, u32[]{:S(2)}) collective-permute-start(bf16[512,512]{1,0:T(8,128)(2,1)S(1)} %get-tuple-element.38.a0), channel_id=1, source_target_pairs={{0,24},{8,0},{16,8},{24,16},{32,56},{40,32},{48,40},{56,48},{64,88... | collective-permute-start | bytes 1572872 | tf_op jit(solution)/shard_map/ppermute | solution.py:306
  18.4 7.9 %collective-permute-start.1 = (bf16[256,256]{1,0:T(8,128)(2,1)}, bf16[256,256]{1,0:T(8,128)(2,1)S(1)}, u32[]{:S(2)}, u32[]{:S(2)}) collective-permute-start(bf16[256,256]{1,0:T(8,128)(2,1)} %get-tuple-element.36), channel_id=1, source_target_pairs={{8,0},{16,8},{24,16},{32,24},{40,32},{48,40},{56,48},{64,56},{72,6... | collective-permute-start | bytes 393224 | tf_op jit(solution)/shard_map/ppermute | solution.py:312
  21.6 23.5 %collective-permute-start.5 = (bf16[512,512]{1,0:T(8,128)(2,1)S(1)}, bf16[512,512]{1,0:T(8,128)(2,1)S(1)}, u32[]{:S(2)}, u32[]{:S(2)}) collective-permute-start(bf16[512,512]{1,0:T(8,128)(2,1)S(1)} %get-tuple-element.46.d0), channel_id=1, source_target_pairs={{0,8},{8,16},{16,24},{24,0},{32,40},{40,48},{48,56},{56,32},{64,72... | collective-permute-start | bytes 1572872 | tf_op jit(solution)/shard_map/ppermute | solution.py:311
  26.3 7.5 %copy-start.3 = (bf16[256,256]{1,0:T(8,128)(2,1)}, bf16[256,256]{1,0:T(8,128)(2,1)S(1)}, u32[]{:S(2)}) copy-start(bf16[256,256]{1,0:T(8,128)(2,1)S(1)} %collective-permute-done.1.back) | copy-start | bytes 393220
  26.3 22.2 %collective-permute-start.6 = (bf16[512,512]{1,0:T(8,128)(2,1)S(1)}, bf16[512,512]{1,0:T(8,128)(2,1)S(1)}, u32[]{:S(2)}, u32[]{:S(2)}) collective-permute-start(bf16[512,512]{1,0:T(8,128)(2,1)S(1)} %get-tuple-element.46.d0), channel_id=1, source_target_pairs={{0,24},{8,0},{16,8},{24,16},{32,56},{40,32},{48,40},{56,48},{64,88... | collective-permute-start | bytes 1572872 | tf_op jit(solution)/shard_map/ppermute | solution.py:313
  33.9 34.4 %copy-start.4 = (bf16[512,512]{1,0:T(8,128)(2,1)}, bf16[512,512]{1,0:T(8,128)(2,1)S(1)}, u32[]{:S(2)}) copy-start(bf16[512,512]{1,0:T(8,128)(2,1)S(1)} %collective-permute-done.3.a1) | copy-start | bytes 1572868
  33.9 34.4 %copy-start.5 = (bf16[512,512]{1,0:T(8,128)(2,1)}, bf16[512,512]{1,0:T(8,128)(2,1)S(1)}, u32[]{:S(2)}) copy-start(bf16[512,512]{1,0:T(8,128)(2,1)S(1)} %collective-permute-done.2.a3) | copy-start | bytes 1572868
  33.9 27.2 %collective-permute-start.4 = (bf16[512,512]{1,0:T(8,128)(2,1)S(1)}, bf16[512,512]{1,0:T(8,128)(2,1)S(1)}, u32[]{:S(2)}, u32[]{:S(2)}) collective-permute-start(bf16[512,512]{1,0:T(8,128)(2,1)S(1)} %collective-permute-done.3.a1), channel_id=1, source_target_pairs={{0,8},{8,16},{16,24},{24,0},{32,40},{40,48},{48,56},{56,32},{64,72... | collective-permute-start | bytes 1572872 | tf_op jit(solution)/shard_map/ppermute | solution.py:314
  37.3 14.1 %collective-permute-start.11 = (bf16[512,256]{1,0:T(8,128)(2,1)}, bf16[512,256]{1,0:T(8,128)(2,1)S(1)}, u32[]{:S(2)}, u32[]{:S(2)}) collective-permute-start(bf16[512,256]{1,0:T(8,128)(2,1)} %get-tuple-element.47), channel_id=1, source_target_pairs={{0,20},{1,17},{2,22},{3,19},{4,16},{5,21},{6,18},{7,23},{8,26},{9,... | collective-permute-start | bytes 786440 | tf_op jit(solution)/shard_map/ppermute | solution.py:318
  44.0 14.5 %collective-permute-start.10 = (bf16[512,256]{1,0:T(8,128)(2,1)}, bf16[512,256]{1,0:T(8,128)(2,1)S(1)}, u32[]{:S(2)}, u32[]{:S(2)}) collective-permute-start(bf16[512,256]{1,0:T(8,128)(2,1)} %get-tuple-element.47), channel_id=1, source_target_pairs={{0,26},{1,31},{2,28},{3,25},{4,30},{5,27},{6,24},{7,29},{8,0},{9,5... | collective-permute-start | bytes 786440 | tf_op jit(solution)/shard_map/ppermute | solution.py:318
  45.0 23.2 %copy-start.6 = (bf16[512,512]{1,0:T(8,128)(2,1)}, bf16[512,512]{1,0:T(8,128)(2,1)S(1)}, u32[]{:S(2)}) copy-start(bf16[512,512]{1,0:T(8,128)(2,1)S(1)} %collective-permute-done.5.d1) | copy-start | bytes 1572868
  45.0 15.6 %collective-permute-start.9 = (bf16[512,256]{1,0:T(8,128)(2,1)}, bf16[512,256]{1,0:T(8,128)(2,1)S(1)}, u32[]{:S(2)}, u32[]{:S(2)}) collective-permute-start(bf16[512,256]{1,0:T(8,128)(2,1)} %get-tuple-element.47), channel_id=1, source_target_pairs={{0,14},{1,11},{2,8},{3,13},{4,10},{5,15},{6,12},{7,9},{8,20},{9,17... | collective-permute-start | bytes 786440 | tf_op jit(solution)/shard_map/ppermute | solution.py:318
  48.5 19.8 %copy-start.7 = (bf16[512,512]{1,0:T(8,128)(2,1)}, bf16[512,512]{1,0:T(8,128)(2,1)S(1)}, u32[]{:S(2)}) copy-start(bf16[512,512]{1,0:T(8,128)(2,1)S(1)} %collective-permute-done.6.d3) | copy-start | bytes 1572868
  48.5 12.1 %collective-permute-start.8 = (bf16[512,256]{1,0:T(8,128)(2,1)}, bf16[512,256]{1,0:T(8,128)(2,1)S(1)}, u32[]{:S(2)}, u32[]{:S(2)}) collective-permute-start(bf16[512,256]{1,0:T(8,128)(2,1)} %get-tuple-element.47), channel_id=1, source_target_pairs={{0,0},{1,5},{2,2},{3,7},{4,4},{5,1},{6,6},{7,3},{8,14},{9,11},{10,... | collective-permute-start | bytes 786440 | tf_op jit(solution)/shard_map/ppermute | solution.py:318
  51.5 16.8 %copy-start.10 = (bf16[512,256]{1,0:T(8,128)(2,1)}, bf16[512,256]{1,0:T(8,128)(2,1)S(1)}, u32[]{:S(2)}) copy-start(bf16[512,256]{1,0:T(8,128)(2,1)S(1)} %collective-permute-done.11.b2) | copy-start | bytes 786436
  51.5 16.8 %collective-permute-start.7 = (bf16[512,512]{1,0:T(8,128)(2,1)S(1)}, bf16[512,512]{1,0:T(8,128)(2,1)S(1)}, u32[]{:S(2)}, u32[]{:S(2)}) collective-permute-start(bf16[512,512]{1,0:T(8,128)(2,1)S(1)} %collective-permute-done.6.d3), channel_id=1, source_target_pairs={{0,24},{8,0},{16,8},{24,16},{32,56},{40,32},{48,40},{56,48},{64,88... | collective-permute-start | bytes 1572872 | tf_op jit(solution)/shard_map/ppermute | solution.py:315
  58.4 9.9 %copy-start.11 = (bf16[512,256]{1,0:T(8,128)(2,1)}, bf16[512,256]{1,0:T(8,128)(2,1)S(1)}, u32[]{:S(2)}) copy-start(bf16[512,256]{1,0:T(8,128)(2,1)S(1)} %collective-permute-done.10.b3) | copy-start | bytes 786436
  58.4 2.8 %collective-permute-start.15 = (bf16[512,256]{1,0:T(8,128)(2,1)S(1)}, bf16[512,256]{1,0:T(8,128)(2,1)S(1)}, u32[]{:S(2)}, u32[]{:S(2)}) collective-permute-start(bf16[512,256]{1,0:T(8,128)(2,1)S(1)} %collective-permute-done.11.b2), channel_id=1, source_target_pairs={{0,1},{1,0},{2,3},{3,2},{4,5},{5,4},{6,7},{7,6},{8,9},{9,8},{10,11... | collective-permute-start | bytes 786440 | tf_op jit(solution)/shard_map/ppermute | solution.py:320
  60.6 7.7 %copy-start.12 = (bf16[512,256]{1,0:T(8,128)(2,1)}, bf16[512,256]{1,0:T(8,128)(2,1)S(1)}, u32[]{:S(2)}) copy-start(bf16[512,256]{1,0:T(8,128)(2,1)S(1)} %collective-permute-done.9.b1) | copy-start | bytes 786436
  60.6 1.5 %collective-permute-start.14 = (bf16[512,256]{1,0:T(8,128)(2,1)S(1)}, bf16[512,256]{1,0:T(8,128)(2,1)S(1)}, u32[]{:S(2)}, u32[]{:S(2)}) collective-permute-start(bf16[512,256]{1,0:T(8,128)(2,1)S(1)} %collective-permute-done.10.b3), channel_id=1, source_target_pairs={{0,1},{1,0},{2,3},{3,2},{4,5},{5,4},{6,7},{7,6},{8,9},{9,8},{10,11... | collective-permute-start | bytes 786440 | tf_op jit(solution)/shard_map/ppermute | solution.py:320
  60.6 1.9 %copy-start.13 = (bf16[512,256]{1,0:T(8,128)(2,1)}, bf16[512,256]{1,0:T(8,128)(2,1)S(1)}, u32[]{:S(2)}) copy-start(bf16[512,256]{1,0:T(8,128)(2,1)S(1)} %collective-permute-done.8.b0) | copy-start | bytes 786436
  60.6 1.9 %collective-permute-start.13 = (bf16[512,256]{1,0:T(8,128)(2,1)S(1)}, bf16[512,256]{1,0:T(8,128)(2,1)S(1)}, u32[]{:S(2)}, u32[]{:S(2)}) collective-permute-start(bf16[512,256]{1,0:T(8,128)(2,1)S(1)} %collective-permute-done.9.b1), channel_id=1, source_target_pairs={{0,1},{1,0},{2,3},{3,2},{4,5},{5,4},{6,7},{7,6},{8,9},{9,8},{10,11... | collective-permute-start | bytes 786440 | tf_op jit(solution)/shard_map/ppermute | solution.py:320
  61.1 7.2 %copy-start.8 = (bf16[512,512]{1,0:T(8,128)(2,1)}, bf16[512,512]{1,0:T(8,128)(2,1)S(1)}, u32[]{:S(2)}) copy-start(bf16[512,512]{1,0:T(8,128)(2,1)S(1)} %collective-permute-done.4.a2) | copy-start | bytes 1572868
  61.1 1.8 %collective-permute-start.12 = (bf16[512,256]{1,0:T(8,128)(2,1)S(1)}, bf16[512,256]{1,0:T(8,128)(2,1)S(1)}, u32[]{:S(2)}, u32[]{:S(2)}) collective-permute-start(bf16[512,256]{1,0:T(8,128)(2,1)S(1)} %collective-permute-done.8.b0), channel_id=1, source_target_pairs={{0,1},{1,0},{2,3},{3,2},{4,5},{5,4},{6,7},{7,6},{8,9},{9,8},{10,11... | collective-permute-start | bytes 786440 | tf_op jit(solution)/shard_map/ppermute | solution.py:320
  61.2 1.7 %copy-start.14 = (bf16[512,256]{1,0:T(8,128)(2,1)}, bf16[512,256]{1,0:T(8,128)(2,1)S(1)}, u32[]{:S(2)}) copy-start(bf16[512,256]{1,0:T(8,128)(2,1)S(1)} %collective-permute-done.15.c2) | copy-start | bytes 786436
  62.1 0.8 copy-start.15
  62.5 0.7 copy-start.16
  63.2 0.7 copy-start.17
  68.3 0.8 copy-start.9

commit v4 on v3

--- a/solution.py
+++ b/solution.py
@@ -313,7 +313,7 @@
     second_right = lax.ppermute(after(second, back), "dp", along_x(-1))
     first_far = lax.ppermute(after(first_left, low), "dp", along_x(1))
     second_far = lax.ppermute(second_right, "dp", along_x(-1))
-    joined, key_gradient, value_gradient = join_gradients(low, high, after(back, first_right, first_left))
+    joined, key_gradient, value_gradient = join_gradients(low, high, after(back, first_right))
 
     mine = [lax.ppermute(joined, ("dp", "tensor"), to_columns(d)) for d in ORDER]
     swap = [(t, t ^ 1) for t in range(2 * NY)]

time: 116 us -> 116 us (level)
  no operation moved by 1% of the time
where the time goes in v4:
time: 116 us; the launch traced here: 115 us
  blocking collectives  38 us (33%)
  starting transfers between devices  33.9 us (29%)
  Pallas kernels  25.8 us (22%)
  waiting for transfers between devices  13.6 us (12%)
  local copies, waits for them, and re-layouts  3.12 us (3%)
    all_to_all x1, blocking collectives, body(): parts = lax.all_to_all(partial, 'dp', 0, 0, tiled=True)  38 us
    ppermute x4, starting transfers between devices, body(): lax.ppermute(joined, ('dp', 'tensor'), to_columns(d))  15.2 us
    pallas_call x1, Pallas kernels, attention(): pl.pallas_call(late_kernel, grid=(1,), in_specs=[wide(1), wide(1), kv(0),...  6.99 us
    pallas_call x1, Pallas kernels, attention(): pl.pallas_call(early_kernel, grid=(1,), in_specs=[wide(0), wide(0), kv(0)...  6.86 us
    ppermute x1, starting transfers between devices, body(): second_far = lax.ppermute(second_right, 'dp', along_x(-1))  6.64 us
    pallas_call x1, Pallas kernels, weight_partial(): pl.pallas_call(weight_kernel, grid=(2 * steps,), in_specs=[low] * 4 + [hi...  6.2 us
    ppermute x1, waiting for transfers between devices, body(): second_far = lax.ppermute(second_right, 'dp', along_x(-1))  4.38 us
    ppermute x1, starting transfers between devices, body(): prior = lax.ppermute(pack_tail(key_rows, value_matrix), 'dp', onward)  3.39 us
  transfers between devices with their start and end apart: 16, of which 7 were waited for; matrix products, arithmetic and copies ran while one was open for 0% of the time, Pallas kernels for 14%

profile of v4, /device:TPU:2, one launch (start us, length us, event | category | flops | bytes accessed | tf_op | source)
XLA Modules:
  0.0 115.3 jit_solution(9000499591491580339)
XLA Ops:
  0.6 1.6 %pack_tail.1 = bf16[256,256]{1,0:T(8,128)(2,1)} custom-call(bf16[512,128]{1,0:T(8,128)(2,1)} %k_hi.3, bf16[512,128]{1,0:T(8,128)(2,1)} %v_hi.3), custom_call_target="tpu_custom_call" | custom-call | tf_op jit(solution)/shard_map/pack_tail/pallas_call | solution.py:153
  2.2 3.4 %collective-permute-start = (bf16[256,256]{1,0:T(8,128)(2,1)}, bf16[256,256]{1,0:T(8,128)(2,1)S(1)}, u32[]{:S(2)}, u32[]{:S(2)}) collective-permute-start(bf16[256,256]{1,0:T(8,128)(2,1)} %pack_tail.1), channel_id=1, source_target_pairs={{0,8},{8,16},{16,24},{24,32},{32,40},{40,48},{48,56},{56,64},{64,7... | collective-permute-start | bytes 393224 | tf_op jit(solution)/shard_map/ppermute | solution.py:301
  5.6 0.0 copy-start
  5.6 1.2 %copy-done = bf16[512,1024]{1,0:T(8,128)(2,1)S(1)} copy-done((bf16[512,1024]{1,0:T(8,128)(2,1)S(1)}, bf16[512,1024]{1,0:T(8,128)(2,1)}, u32[]{:S(2)}) %copy-start) | copy-done | bytes 1048600
  6.8 0.3 split_inputs.1
  7.2 2.4 %collective-permute-done.k_lo.v_lo = bf16[256,256]{1,0:T(8,128)(2,1)S(1)} collective-permute-done((bf16[256,256]{1,0:T(8,128)(2,1)}, bf16[256,256]{1,0:T(8,128)(2,1)S(1)}, u32[]{:S(2)}, u32[]{:S(2)}) %collective-permute-start) | collective-permute-done | bytes 131104 | tf_op jit(solution)/shard_map/ppermute | solution.py:301
  9.5 0.0 collective-permute-start.2
  9.5 2.0 %collective-permute-start.3 = (bf16[512,512]{1,0:T(8,128)(2,1)S(1)}, bf16[512,512]{1,0:T(8,128)(2,1)S(1)}, u32[]{:S(2)}, u32[]{:S(2)}) collective-permute-start(bf16[512,512]{1,0:T(8,128)(2,1)S(1)} %get-tuple-element.38.a0), channel_id=1, source_target_pairs={{0,8},{8,16},{16,24},{24,0},{32,40},{40,48},{48,56},{56,32},{64,72... | collective-permute-start | bytes 1572872 | tf_op jit(solution)/shard_map/ppermute | solution.py:305
  11.5 6.9 %attend_early.1 = (bf16[512,1024]{1,0:T(8,128)(2,1)}, bf16[512,1024]{1,0:T(8,128)(2,1)}, f32[8,512]{1,0:T(8,128)}, f32[256,128]{1,0:T(8,128)}, f32[256,128]{1,0:T(8,128)}, /*index=5*/bf16[256,256]{1,0:T(8,128)(2,1)}) custom-call(bf16[512,1024]{1,0:T(8,128)(2,1)} %q.3, bf16[512,1024]{1,0:T(8,128)(2,1)} %g.3, bf16[256,256]{1,0:T(8,128)(2,1)} %copy-done.18, ...), custom_call_target="tpu_custom_call" | custom-call | flops 1207959552 | bytes 33554432 | tf_op jit(solution)/shard_map/attend_early/pallas_call | solution.py:119
  18.4 0.0 copy-done.1
  18.4 3.2 %collective-permute-start.1 = (bf16[256,256]{1,0:T(8,128)(2,1)}, bf16[256,256]{1,0:T(8,128)(2,1)S(1)}, u32[]{:S(2)}, u32[]{:S(2)}) collective-permute-start(bf16[256,256]{1,0:T(8,128)(2,1)} %get-tuple-element.36), channel_id=1, source_target_pairs={{8,0},{16,8},{24,16},{32,24},{40,32},{48,40},{56,48},{64,56},{72,6... | collective-permute-start | bytes 393224 | tf_op jit(solution)/shard_map/ppermute | solution.py:312
  21.6 0.8 collective-permute-start.5
  22.4 3.1 %collective-permute-done.1.back = bf16[256,256]{1,0:T(8,128)(2,1)S(1)} collective-permute-done((bf16[256,256]{1,0:T(8,128)(2,1)}, bf16[256,256]{1,0:T(8,128)(2,1)S(1)}, u32[]{:S(2)}, u32[]{:S(2)}) %collective-permute-start.1) | collective-permute-done | bytes 131104 | tf_op jit(solution)/shard_map/ppermute | solution.py:312
  25.5 1.3 %collective-permute-start.6 = (bf16[512,512]{1,0:T(8,128)(2,1)S(1)}, bf16[512,512]{1,0:T(8,128)(2,1)S(1)}, u32[]{:S(2)}, u32[]{:S(2)}) collective-permute-start(bf16[512,512]{1,0:T(8,128)(2,1)S(1)} %get-tuple-element.46.d0), channel_id=1, source_target_pairs={{0,24},{8,0},{16,8},{24,16},{32,56},{40,32},{48,40},{56,48},{64,88... | collective-permute-start | bytes 1572872 | tf_op jit(solution)/shard_map/ppermute | solution.py:313
  26.7 7.0 %attend_late.1 = (bf16[512,1024]{1,0:T(8,128)(2,1)}, bf16[512,1024]{1,0:T(8,128)(2,1)}, f32[8,512]{1,0:T(8,128)}, bf16[256,256]{1,0:T(8,128)(2,1)}, f32[256,256]{1,0:T(8,128)}) custom-call(bf16[512,1024]{1,0:T(8,128)(2,1)} %q.3, bf16[512,1024]{1,0:T(8,128)(2,1)} %g.3, ...), custom_call_target="tpu_custom_call", output_to_operand_aliasing={{0}: (9, {}), {1}: (10, {}), {2}: (11, {})} | custom-call | flops 1207959552 | bytes 33554432 | tf_op jit(solution)/shard_map/attend_late/pallas_call | solution.py:131
  33.7 0.0 collective-permute-done.2.a3
  33.8 0.0 collective-permute-done.3.a1
  33.8 0.0 copy-start.5
  33.8 0.8 collective-permute-start.4
  34.6 1.9 %join_gradients.1 = (bf16[512,256]{1,0:T(8,128)(2,1)}, bf16[512,128]{1,0:T(8,128)(2,1)}, bf16[512,128]{1,0:T(8,128)(2,1)}) custom-call(bf16[256,256]{1,0:T(8,128)(2,1)} %get-tuple-element.34.low, f32[256,256]{1,0:T(8,128)} %get-tuple-element.35.high, bf16[256,256]{1,0:T(8,128)(2,1)} %copy-done.3), custom_call_target="tpu_custom_call" | custom-call | tf_op jit(solution)/shard_map/join_gradients/pallas_call | solution.py:199
  36.5 7.7 %collective-permute-start.11 = (bf16[512,256]{1,0:T(8,128)(2,1)}, bf16[512,256]{1,0:T(8,128)(2,1)S(1)}, u32[]{:S(2)}, u32[]{:S(2)}) collective-permute-start(bf16[512,256]{1,0:T(8,128)(2,1)} %get-tuple-element.47), channel_id=1, source_target_pairs={{0,20},{1,17},{2,22},{3,19},{4,16},{5,21},{6,18},{7,23},{8,26},{9,... | collective-permute-start | bytes 786440 | tf_op jit(solution)/shard_map/ppermute | solution.py:318
  44.1 1.1 collective-permute-start.10
  45.2 0.0 collective-permute-done.5.d1
  45.2 3.5 %collective-permute-start.9 = (bf16[512,256]{1,0:T(8,128)(2,1)}, bf16[512,256]{1,0:T(8,128)(2,1)S(1)}, u32[]{:S(2)}, u32[]{:S(2)}) collective-permute-start(bf16[512,256]{1,0:T(8,128)(2,1)} %get-tuple-element.47), channel_id=1, source_target_pairs={{0,14},{1,11},{2,8},{3,13},{4,10},{5,15},{6,12},{7,9},{8,20},{9,17... | collective-permute-start | bytes 786440 | tf_op jit(solution)/shard_map/ppermute | solution.py:318
  48.7 0.0 collective-permute-done.6.d3
  48.7 3.0 %collective-permute-start.8 = (bf16[512,256]{1,0:T(8,128)(2,1)}, bf16[512,256]{1,0:T(8,128)(2,1)S(1)}, u32[]{:S(2)}, u32[]{:S(2)}) collective-permute-start(bf16[512,256]{1,0:T(8,128)(2,1)} %get-tuple-element.47), channel_id=1, source_target_pairs={{0,0},{1,5},{2,2},{3,7},{4,4},{5,1},{6,6},{7,3},{8,14},{9,11},{10,... | collective-permute-start | bytes 786440 | tf_op jit(solution)/shard_map/ppermute | solution.py:318
  51.7 0.0 collective-permute-done.11.b2
  51.7 6.6 %collective-permute-start.7 = (bf16[512,512]{1,0:T(8,128)(2,1)S(1)}, bf16[512,512]{1,0:T(8,128)(2,1)S(1)}, u32[]{:S(2)}, u32[]{:S(2)}) collective-permute-start(bf16[512,512]{1,0:T(8,128)(2,1)S(1)} %collective-permute-done.6.d3), channel_id=1, source_target_pairs={{0,24},{8,0},{16,8},{24,16},{32,56},{40,32},{48,40},{56,48},{64,88... | collective-permute-start | bytes 1572872 | tf_op jit(solution)/shard_map/ppermute | solution.py:315
  58.3 0.0 collective-permute-done.10.b3
  58.3 0.0 collective-permute-start.15
  58.3 2.2 %collective-permute-done.9.b1 = bf16[512,256]{1,0:T(8,128)(2,1)S(1)} collective-permute-done((bf16[512,256]{1,0:T(8,128)(2,1)}, bf16[512,256]{1,0:T(8,128)(2,1)S(1)}, u32[]{:S(2)}, u32[]{:S(2)}) %collective-permute-start.9) | collective-permute-done | bytes 262176 | tf_op jit(solution)/shard_map/ppermute | solution.py:318
  60.5 0.0 collective-permute-start.14
  60.5 0.0 collective-permute-done.8.b0
  60.5 0.0 copy-start.13
  60.5 0.5 collective-permute-start.13
  61.0 0.0 collective-permute-done.4.a2
  61.0 0.1 collective-permute-start.12
  61.1 0.0 collective-permute-done.15.c2
  61.1 0.9 collective-permute-done.14.c3
  62.0 0.4 collective-permute-done.13.c1
  62.4 0.4 collective-permute-done.12.c0
  62.8 0.3 copy-done.16
  63.1 0.7 copy-done.17
  63.8 4.4 %collective-permute-done.7.d2 = bf16[512,512]{1,0:T(8,128)(2,1)S(1)} collective-permute-done((bf16[512,512]{1,0:T(8,128)(2,1)S(1)}, bf16[512,512]{1,0:T(8,128)(2,1)S(1)}, u32[]{:S(2)}, u32[]{:S(2)}) %collective-permute-start.7) | collective-permute-done | bytes 524320 | tf_op jit(solution)/shard_map/ppermute | solution.py:315
  68.3 0.8 copy-done.9
  69.1 6.2 %weight_partial.1 = bf16[1024,512]{1,0:T(8,128)(2,1)} custom-call(bf16[512,512]{1,0:T(8,128)(2,1)} %copy-done.1, bf16[512,512]{1,0:T(8,128)(2,1)} %copy-done.5, bf16[512,512]{1,0:T(8,128)(2,1)} %copy-done.4, bf16[512,512]{1,0:T(8,128)(2,1)} %copy-done.8, bf16[512,512]{1,0:T(8,128)(2,1)} %copy-done.2, bf16[512,512]{1,0:T(8,128)(2,1)} %copy-done.6, ...), custom_call_target="tpu_custom_call" | custom-call | flops 2147483648 | bytes 8388608 | tf_op jit(solution)/shard_map/weight_partial/pallas_call | solution.py:238
  75.3 38.0 %all_to_all.9.parts = bf16[32,32,512]{2,1,0:T(8,128)(2,1)} all-to-all(bf16[32,32,512]{2,1,0:T(8,128)(2,1)} %bitcast.2), channel_id=1, replica_groups=mesh['dp'=32,'tensor'=8] {'dp'}, dimensions={0} | all-to-all | bytes 2097152 | tf_op jit(solution)/shard_map/all_to_all | solution.py:324
  113.3 2.1 %sum_parts.1 = f32[32,2048]{1,0:T(8,128)} custom-call(bf16[32,32,512]{2,1,0:T(8,128)(2,1)} %all_to_all.9.parts), custom_call_target="tpu_custom_call" | custom-call | flops 524288 | bytes 2097152 | tf_op jit(solution)/shard_map/sum_parts/pallas_call | solution.py:264
  (30 shorter events, 0.1 us)
Async XLA Ops:
  2.2 7.3 %collective-permute-start = (bf16[256,256]{1,0:T(8,128)(2,1)}, bf16[256,256]{1,0:T(8,128)(2,1)S(1)}, u32[]{:S(2)}, u32[]{:S(2)}) collective-permute-start(bf16[256,256]{1,0:T(8,128)(2,1)} %pack_tail.1), channel_id=1, source_target_pairs={{0,8},{8,16},{16,24},{24,32},{32,40},{40,48},{48,56},{56,64},{64,7... | collective-permute-start | bytes 393224 | tf_op jit(solution)/shard_map/ppermute | solution.py:301
  5.6 1.2 %copy-start = (bf16[512,1024]{1,0:T(8,128)(2,1)S(1)}, bf16[512,1024]{1,0:T(8,128)(2,1)}, u32[]{:S(2)}) copy-start(bf16[512,1024]{1,0:T(8,128)(2,1)} %x.1) | copy-start | bytes 3145732
  7.1 11.3 %copy-start.1 = (bf16[512,512]{1,0:T(8,128)(2,1)}, bf16[512,512]{1,0:T(8,128)(2,1)S(1)}, u32[]{:S(2)}) copy-start(bf16[512,512]{1,0:T(8,128)(2,1)S(1)} %get-tuple-element.38.a0) | copy-start | bytes 1572868
  7.1 18.3 %copy-start.2 = (bf16[512,512]{1,0:T(8,128)(2,1)}, bf16[512,512]{1,0:T(8,128)(2,1)S(1)}, u32[]{:S(2)}) copy-start(bf16[512,512]{1,0:T(8,128)(2,1)S(1)} %get-tuple-element.46.d0) | copy-start | bytes 1572868
  9.5 2.0 %copy-start.18 = (bf16[256,256]{1,0:T(8,128)(2,1)}, bf16[256,256]{1,0:T(8,128)(2,1)S(1)}, u32[]{:S(2)}) copy-start(bf16[256,256]{1,0:T(8,128)(2,1)S(1)} %collective-permute-done.k_lo.v_lo) | copy-start | bytes 393220
  9.5 24.2 %collective-permute-start.2 = (bf16[512,512]{1,0:T(8,128)(2,1)S(1)}, bf16[512,512]{1,0:T(8,128)(2,1)S(1)}, u32[]{:S(2)}, u32[]{:S(2)}) collective-permute-start(bf16[512,512]{1,0:T(8,128)(2,1)S(1)} %get-tuple-element.38.a0), channel_id=1, source_target_pairs={{0,24},{8,0},{16,8},{24,16},{32,56},{40,32},{48,40},{56,48},{64,88... | collective-permute-start | bytes 1572872 | tf_op jit(solution)/shard_map/ppermute | solution.py:306
  9.5 24.2 %collective-permute-start.3 = (bf16[512,512]{1,0:T(8,128)(2,1)S(1)}, bf16[512,512]{1,0:T(8,128)(2,1)S(1)}, u32[]{:S(2)}, u32[]{:S(2)}) collective-permute-start(bf16[512,512]{1,0:T(8,128)(2,1)S(1)} %get-tuple-element.38.a0), channel_id=1, source_target_pairs={{0,8},{8,16},{16,24},{24,0},{32,40},{40,48},{48,56},{56,32},{64,72... | collective-permute-start | bytes 1572872 | tf_op jit(solution)/shard_map/ppermute | solution.py:305
  18.4 7.1 %collective-permute-start.1 = (bf16[256,256]{1,0:T(8,128)(2,1)}, bf16[256,256]{1,0:T(8,128)(2,1)S(1)}, u32[]{:S(2)}, u32[]{:S(2)}) collective-permute-start(bf16[256,256]{1,0:T(8,128)(2,1)} %get-tuple-element.36), channel_id=1, source_target_pairs={{8,0},{16,8},{24,16},{32,24},{40,32},{48,40},{56,48},{64,56},{72,6... | collective-permute-start | bytes 393224 | tf_op jit(solution)/shard_map/ppermute | solution.py:312
  21.6 23.6 %collective-permute-start.5 = (bf16[512,512]{1,0:T(8,128)(2,1)S(1)}, bf16[512,512]{1,0:T(8,128)(2,1)S(1)}, u32[]{:S(2)}, u32[]{:S(2)}) collective-permute-start(bf16[512,512]{1,0:T(8,128)(2,1)S(1)} %get-tuple-element.46.d0), channel_id=1, source_target_pairs={{0,8},{8,16},{16,24},{24,0},{32,40},{40,48},{48,56},{56,32},{64,72... | collective-permute-start | bytes 1572872 | tf_op jit(solution)/shard_map/ppermute | solution.py:311
  25.5 8.3 %copy-start.3 = (bf16[256,256]{1,0:T(8,128)(2,1)}, bf16[256,256]{1,0:T(8,128)(2,1)S(1)}, u32[]{:S(2)}) copy-start(bf16[256,256]{1,0:T(8,128)(2,1)S(1)} %collective-permute-done.1.back) | copy-start | bytes 393220
  25.5 23.2 %collective-permute-start.6 = (bf16[512,512]{1,0:T(8,128)(2,1)S(1)}, bf16[512,512]{1,0:T(8,128)(2,1)S(1)}, u32[]{:S(2)}, u32[]{:S(2)}) collective-permute-start(bf16[512,512]{1,0:T(8,128)(2,1)S(1)} %get-tuple-element.46.d0), channel_id=1, source_target_pairs={{0,24},{8,0},{16,8},{24,16},{32,56},{40,32},{48,40},{56,48},{64,88... | collective-permute-start | bytes 1572872 | tf_op jit(solution)/shard_map/ppermute | solution.py:313
  33.7 34.5 %copy-start.4 = (bf16[512,512]{1,0:T(8,128)(2,1)}, bf16[512,512]{1,0:T(8,128)(2,1)S(1)}, u32[]{:S(2)}) copy-start(bf16[512,512]{1,0:T(8,128)(2,1)S(1)} %collective-permute-done.2.a3) | copy-start | bytes 1572868
  33.8 34.5 %copy-start.5 = (bf16[512,512]{1,0:T(8,128)(2,1)}, bf16[512,512]{1,0:T(8,128)(2,1)S(1)}, u32[]{:S(2)}) copy-start(bf16[512,512]{1,0:T(8,128)(2,1)S(1)} %collective-permute-done.3.a1) | copy-start | bytes 1572868
  33.8 27.3 %collective-permute-start.4 = (bf16[512,512]{1,0:T(8,128)(2,1)S(1)}, bf16[512,512]{1,0:T(8,128)(2,1)S(1)}, u32[]{:S(2)}, u32[]{:S(2)}) collective-permute-start(bf16[512,512]{1,0:T(8,128)(2,1)S(1)} %collective-permute-done.3.a1), channel_id=1, source_target_pairs={{0,8},{8,16},{16,24},{24,0},{32,40},{40,48},{48,56},{56,32},{64,72... | collective-permute-start | bytes 1572872 | tf_op jit(solution)/shard_map/ppermute | solution.py:314
  36.5 15.2 %collective-permute-start.11 = (bf16[512,256]{1,0:T(8,128)(2,1)}, bf16[512,256]{1,0:T(8,128)(2,1)S(1)}, u32[]{:S(2)}, u32[]{:S(2)}) collective-permute-start(bf16[512,256]{1,0:T(8,128)(2,1)} %get-tuple-element.47), channel_id=1, source_target_pairs={{0,20},{1,17},{2,22},{3,19},{4,16},{5,21},{6,18},{7,23},{8,26},{9,... | collective-permute-start | bytes 786440 | tf_op jit(solution)/shard_map/ppermute | solution.py:318
  44.1 14.2 %collective-permute-start.10 = (bf16[512,256]{1,0:T(8,128)(2,1)}, bf16[512,256]{1,0:T(8,128)(2,1)S(1)}, u32[]{:S(2)}, u32[]{:S(2)}) collective-permute-start(bf16[512,256]{1,0:T(8,128)(2,1)} %get-tuple-element.47), channel_id=1, source_target_pairs={{0,26},{1,31},{2,28},{3,25},{4,30},{5,27},{6,24},{7,29},{8,0},{9,5... | collective-permute-start | bytes 786440 | tf_op jit(solution)/shard_map/ppermute | solution.py:318
  45.2 23.0 %copy-start.6 = (bf16[512,512]{1,0:T(8,128)(2,1)}, bf16[512,512]{1,0:T(8,128)(2,1)S(1)}, u32[]{:S(2)}) copy-start(bf16[512,512]{1,0:T(8,128)(2,1)S(1)} %collective-permute-done.5.d1) | copy-start | bytes 1572868
  45.2 15.3 %collective-permute-start.9 = (bf16[512,256]{1,0:T(8,128)(2,1)}, bf16[512,256]{1,0:T(8,128)(2,1)S(1)}, u32[]{:S(2)}, u32[]{:S(2)}) collective-permute-start(bf16[512,256]{1,0:T(8,128)(2,1)} %get-tuple-element.47), channel_id=1, source_target_pairs={{0,14},{1,11},{2,8},{3,13},{4,10},{5,15},{6,12},{7,9},{8,20},{9,17... | collective-permute-start | bytes 786440 | tf_op jit(solution)/shard_map/ppermute | solution.py:318
  48.7 19.6 %copy-start.7 = (bf16[512,512]{1,0:T(8,128)(2,1)}, bf16[512,512]{1,0:T(8,128)(2,1)S(1)}, u32[]{:S(2)}) copy-start(bf16[512,512]{1,0:T(8,128)(2,1)S(1)} %collective-permute-done.6.d3) | copy-start | bytes 1572868
  48.7 11.8 %collective-permute-start.8 = (bf16[512,256]{1,0:T(8,128)(2,1)}, bf16[512,256]{1,0:T(8,128)(2,1)S(1)}, u32[]{:S(2)}, u32[]{:S(2)}) collective-permute-start(bf16[512,256]{1,0:T(8,128)(2,1)} %get-tuple-element.47), channel_id=1, source_target_pairs={{0,0},{1,5},{2,2},{3,7},{4,4},{5,1},{6,6},{7,3},{8,14},{9,11},{10,... | collective-permute-start | bytes 786440 | tf_op jit(solution)/shard_map/ppermute | solution.py:318
  51.7 16.6 %copy-start.10 = (bf16[512,256]{1,0:T(8,128)(2,1)}, bf16[512,256]{1,0:T(8,128)(2,1)S(1)}, u32[]{:S(2)}) copy-start(bf16[512,256]{1,0:T(8,128)(2,1)S(1)} %collective-permute-done.11.b2) | copy-start | bytes 786436
  51.7 16.6 %collective-permute-start.7 = (bf16[512,512]{1,0:T(8,128)(2,1)S(1)}, bf16[512,512]{1,0:T(8,128)(2,1)S(1)}, u32[]{:S(2)}, u32[]{:S(2)}) collective-permute-start(bf16[512,512]{1,0:T(8,128)(2,1)S(1)} %collective-permute-done.6.d3), channel_id=1, source_target_pairs={{0,24},{8,0},{16,8},{24,16},{32,56},{40,32},{48,40},{56,48},{64,88... | collective-permute-start | bytes 1572872 | tf_op jit(solution)/shard_map/ppermute | solution.py:315
  58.3 9.9 %copy-start.11 = (bf16[512,256]{1,0:T(8,128)(2,1)}, bf16[512,256]{1,0:T(8,128)(2,1)S(1)}, u32[]{:S(2)}) copy-start(bf16[512,256]{1,0:T(8,128)(2,1)S(1)} %collective-permute-done.10.b3) | copy-start | bytes 786436
  58.3 2.8 %collective-permute-start.15 = (bf16[512,256]{1,0:T(8,128)(2,1)S(1)}, bf16[512,256]{1,0:T(8,128)(2,1)S(1)}, u32[]{:S(2)}, u32[]{:S(2)}) collective-permute-start(bf16[512,256]{1,0:T(8,128)(2,1)S(1)} %collective-permute-done.11.b2), channel_id=1, source_target_pairs={{0,1},{1,0},{2,3},{3,2},{4,5},{5,4},{6,7},{7,6},{8,9},{9,8},{10,11... | collective-permute-start | bytes 786440 | tf_op jit(solution)/shard_map/ppermute | solution.py:320
  60.5 7.8 %copy-start.12 = (bf16[512,256]{1,0:T(8,128)(2,1)}, bf16[512,256]{1,0:T(8,128)(2,1)S(1)}, u32[]{:S(2)}) copy-start(bf16[512,256]{1,0:T(8,128)(2,1)S(1)} %collective-permute-done.9.b1) | copy-start | bytes 786436
  60.5 1.5 %collective-permute-start.14 = (bf16[512,256]{1,0:T(8,128)(2,1)S(1)}, bf16[512,256]{1,0:T(8,128)(2,1)S(1)}, u32[]{:S(2)}, u32[]{:S(2)}) collective-permute-start(bf16[512,256]{1,0:T(8,128)(2,1)S(1)} %collective-permute-done.10.b3), channel_id=1, source_target_pairs={{0,1},{1,0},{2,3},{3,2},{4,5},{5,4},{6,7},{7,6},{8,9},{9,8},{10,11... | collective-permute-start | bytes 786440 | tf_op jit(solution)/shard_map/ppermute | solution.py:320
  60.5 1.9 %copy-start.13 = (bf16[512,256]{1,0:T(8,128)(2,1)}, bf16[512,256]{1,0:T(8,128)(2,1)S(1)}, u32[]{:S(2)}) copy-start(bf16[512,256]{1,0:T(8,128)(2,1)S(1)} %collective-permute-done.8.b0) | copy-start | bytes 786436
  60.5 1.9 %collective-permute-start.13 = (bf16[512,256]{1,0:T(8,128)(2,1)S(1)}, bf16[512,256]{1,0:T(8,128)(2,1)S(1)}, u32[]{:S(2)}, u32[]{:S(2)}) collective-permute-start(bf16[512,256]{1,0:T(8,128)(2,1)S(1)} %collective-permute-done.9.b1), channel_id=1, source_target_pairs={{0,1},{1,0},{2,3},{3,2},{4,5},{5,4},{6,7},{7,6},{8,9},{9,8},{10,11... | collective-permute-start | bytes 786440 | tf_op jit(solution)/shard_map/ppermute | solution.py:320
  61.0 7.3 %copy-start.8 = (bf16[512,512]{1,0:T(8,128)(2,1)}, bf16[512,512]{1,0:T(8,128)(2,1)S(1)}, u32[]{:S(2)}) copy-start(bf16[512,512]{1,0:T(8,128)(2,1)S(1)} %collective-permute-done.4.a2) | copy-start | bytes 1572868
  61.0 1.8 %collective-permute-start.12 = (bf16[512,256]{1,0:T(8,128)(2,1)S(1)}, bf16[512,256]{1,0:T(8,128)(2,1)S(1)}, u32[]{:S(2)}, u32[]{:S(2)}) collective-permute-start(bf16[512,256]{1,0:T(8,128)(2,1)S(1)} %collective-permute-done.8.b0), channel_id=1, source_target_pairs={{0,1},{1,0},{2,3},{3,2},{4,5},{5,4},{6,7},{7,6},{8,9},{9,8},{10,11... | collective-permute-start | bytes 786440 | tf_op jit(solution)/shard_map/ppermute | solution.py:320
  61.1 1.7 %copy-start.14 = (bf16[512,256]{1,0:T(8,128)(2,1)}, bf16[512,256]{1,0:T(8,128)(2,1)S(1)}, u32[]{:S(2)}) copy-start(bf16[512,256]{1,0:T(8,128)(2,1)S(1)} %collective-permute-done.15.c2) | copy-start | bytes 786436
  62.0 0.8 copy-start.15
  62.4 0.7 copy-start.16
  63.1 0.7 copy-start.17
  68.3 0.8 copy-start.9
